TPU v7x, 256 devices: a whole 4x4x8 slice. The times are simulated.
256 devices in a mesh: ctx: 32 (over y, z), head: 8 (over x, core).
Axes of the slice: x: 4, y: 4, z: 8, core: 2. Of those that a mesh axis runs over, the one named last changes fastest.
Arguments:
- q_raw: bfloat16 [8192, 5120], P('ctx', 'head'), may hold values from -500 to 500
- k_raw: bfloat16 [8192, 5120], P('ctx', 'head'), may hold values from -500 to 500
- values: bfloat16 [8192, 5120], P('ctx', 'head'), may hold values from -6 to 6
- grad_out: bfloat16 [8192, 5120], P('ctx', 'head'), may hold values from -50 to 50
- gain_q: float32 [128], replicated, may hold values from 0.5 to 5
- gain_k: float32 [128], replicated, may hold values from 0.5 to 5
- pair_blocks: int32 [32, 2], P('ctx'), may hold values from 0 to 31, as said below
- pair_count: int32 [32], P('ctx'), may hold values from 0 to 2
Outputs:
- grad_q: bfloat16 [8192, 5120], P('ctx', 'head')
- grad_k: bfloat16 [8192, 5120], P('ctx', 'head')
- grad_v: bfloat16 [8192, 5120], P('ctx', 'head')
- grad_gain_q: float32 [128], replicated
- grad_gain_k: float32 [128], replicated
Inputs may be any that keep to these rules, and one draw needn't show every extreme that they name: `pair_blocks`: row a lists each of the 2 blocks a XOR 2^i (i < 2) once, in some order. Its first pair_count[a] entries are the active partners of block a, each of them a XOR 2^i for an i at which bit i of a is 0: a pair is listed only at its lower block and is active in both directions.
All inputs are finite; a program needn't handle non-finite values.
Results may differ from a plain program's by a relative error of at most 0.015.
The roundings to bfloat16 on the way count: a program that leaves them out, or rounds other values in their place, can miss the bound.
Values may be sent and summed in bfloat16 or wider, within the bound.
A program may use at most 64 MiB of HBM per device.

v0:
```python
import math

import jax
import jax.numpy as jnp
from jax import lax
from jax.sharding import PartitionSpec as P

HEAD_DIM = 128
BITS = 2


FLOOR_LOG = -1e30


def from_partner(block, axis, distance):
    count = lax.axis_size(axis)
    route = []
    for low in range(count):
        high = low | 1 << distance
        if high != low and high < count:
            route += [(low, high), (high, low)]
    return lax.ppermute(block, axis, route)


def head_norm(raw_rows, gain):
    raw_float = raw_rows.astype(jnp.float32).reshape(raw_rows.shape[0], -1, HEAD_DIM)
    inverse = lax.rsqrt(jnp.mean(raw_float * raw_float, axis=2, keepdims=True) + 1e-06)
    return (raw_float, inverse, (raw_float * inverse * gain).astype(jnp.bfloat16))


def norm_back(raw_float, inverse, gain, grad_normed):
    gain_grad = gain * grad_normed
    inner = jnp.sum(raw_float * gain_grad, axis=2, keepdims=True)
    return inverse * gain_grad - raw_float * inverse * inverse * inverse * inner / HEAD_DIM


def forward_part(query_rows, key_rows, value_rows, factor):
    scores = (
        jnp.einsum("thd,shd->hts", query_rows, key_rows, preferred_element_type=jnp.float32)
        * factor
    )
    largest = jnp.max(scores, axis=2)
    log_total = largest + jnp.log(jnp.sum(jnp.exp(scores - largest[:, :, None]), axis=2))
    weights = jnp.exp(scores - log_total[:, :, None]).astype(jnp.bfloat16)
    partial_out = jnp.einsum(
        "hts,shd->thd", weights, value_rows, preferred_element_type=jnp.float32
    )
    return (log_total, partial_out)


def combine(log_parts, out_parts):
    stacked = jnp.stack(log_parts)
    largest = jnp.max(stacked, axis=0)
    log_total = largest + jnp.log(jnp.sum(jnp.exp(stacked - largest), axis=0))
    merged = jnp.zeros_like(out_parts[0])
    for part_log, part_out in zip(log_parts, out_parts):
        merged = merged + jnp.exp(part_log - log_total).T[:, :, None] * part_out
    return (log_total, merged)


def both_sides(query_rows, key_rows, value_rows, grad_rows, log_total, row_dot, factor):
    scores = (
        jnp.einsum("thd,shd->hts", query_rows, key_rows, preferred_element_type=jnp.float32)
        * factor
    )
    weights = jnp.exp(scores - log_total[:, :, None])
    grad_value = jnp.einsum(
        "hts,thd->shd", weights.astype(jnp.bfloat16), grad_rows, preferred_element_type=jnp.float32
    )
    grad_prob = jnp.einsum(
        "thd,shd->hts", grad_rows, value_rows, preferred_element_type=jnp.float32
    )
    grad_score = (weights * (grad_prob - row_dot[:, :, None]) * factor).astype(jnp.bfloat16)
    grad_query = jnp.einsum(
        "hts,shd->thd", grad_score, key_rows, preferred_element_type=jnp.float32
    )
    grad_key = jnp.einsum(
        "hts,thd->shd", grad_score, query_rows, preferred_element_type=jnp.float32
    )
    return (grad_query, grad_key, grad_value)


def is_listed(table_blocks, table_count, first_row, owner, target):
    row_ids = first_row + jnp.arange(table_blocks.shape[0], dtype=jnp.int32)
    slot_live = jnp.arange(table_blocks.shape[1], dtype=jnp.int32)[None, :] < table_count[:, None]
    hits = slot_live & (table_blocks == target) & (row_ids == owner)[:, None]
    return jnp.any(hits)


def body(q_raw, k_raw, values, grad_out, gain_q, gain_k, pair_blocks, pair_count):
    tokens_here = q_raw.shape[0]
    factor = 1.0 / math.sqrt(HEAD_DIM)
    q_float, q_inverse, query = head_norm(q_raw, gain_q)
    k_float, k_inverse, keys_here = head_norm(k_raw, gain_k)
    heads_here = query.shape[1]
    value_rows = values.reshape(tokens_here, heads_here, HEAD_DIM)
    grad_rows = grad_out.reshape(tokens_here, heads_here, HEAD_DIM)
    place = lax.axis_index("ctx")
    empty_log = jnp.full((heads_here, tokens_here), FLOOR_LOG, jnp.float32)
    empty_out = jnp.zeros((tokens_here, heads_here, HEAD_DIM), jnp.float32)
    empty_grad = jnp.zeros((tokens_here, heads_here, HEAD_DIM), jnp.bfloat16)
    diag_log, diag_out = forward_part(query, keys_here, value_rows, factor)
    log_parts = [diag_log]
    out_parts = [diag_out]
    fetched = []
    run_flags = []
    exec_flags = []
    for bit_index in range(BITS):
        bit_mask = 1 << bit_index
        partner = jnp.bitwise_xor(place, bit_mask)
        lower_side = jnp.bitwise_and(place, bit_mask) == 0
        listed_here = lower_side & is_listed(pair_blocks, pair_count, place, place, partner)
        flag_sent = jnp.where(listed_here, 1.0, 0.0).astype(jnp.bfloat16).reshape(1)
        received = from_partner(
            (query, keys_here, value_rows, grad_rows, flag_sent), "ctx", bit_index
        )
        pair_on = jnp.where(lower_side, listed_here, received[4][0] > 0.5)
        if bit_index % 2 == 0:
            executes = lower_side
        else:
            executes = jnp.logical_not(lower_side)
        runs_here = executes & pair_on

        def forward_both():
            own_log, own_out = forward_part(query, received[1], received[2], factor)
            far_log, far_out = forward_part(received[0], keys_here, value_rows, factor)
            return (own_log, own_out, far_log, far_out)

        def forward_none():
            return (empty_log, empty_out, empty_log, empty_out)

        own_log, own_out, far_log, far_out = lax.cond(runs_here, forward_both, forward_none)
        returned = from_partner((far_out, far_log), "ctx", bit_index)
        log_parts.append(jnp.where(executes, own_log, returned[1]))
        out_parts.append(jnp.where(executes, own_out, returned[0]))
        fetched.append(received)
        run_flags.append(runs_here)
        exec_flags.append(executes)
    log_total, merged = combine(log_parts, out_parts)
    row_dot = jnp.sum(grad_rows.astype(jnp.float32) * merged, axis=2).T
    grad_q_sum, grad_k_sum, grad_v_sum = both_sides(
        query, keys_here, value_rows, grad_rows, log_total, row_dot, factor
    )
    for bit_index in range(BITS):
        received = fetched[bit_index]
        stats = from_partner((log_total, row_dot), "ctx", bit_index)

        def backward_both():
            near_q, far_k, far_v = both_sides(
                query, received[1], received[2], grad_rows, log_total, row_dot, factor
            )
            far_q, near_k, near_v = both_sides(
                received[0], keys_here, value_rows, received[3], stats[0], stats[1], factor
            )
            return (
                near_q.astype(jnp.bfloat16),
                near_k.astype(jnp.bfloat16),
                near_v.astype(jnp.bfloat16),
                far_q.astype(jnp.bfloat16),
                far_k.astype(jnp.bfloat16),
                far_v.astype(jnp.bfloat16),
            )

        def backward_none():
            return (empty_grad, empty_grad, empty_grad, empty_grad, empty_grad, empty_grad)

        near_q, near_k, near_v, far_q, far_k, far_v = lax.cond(
            run_flags[bit_index], backward_both, backward_none
        )
        returned = from_partner((far_q, far_k, far_v), "ctx", bit_index)
        executes = exec_flags[bit_index]
        grad_q_sum = grad_q_sum + jnp.where(executes, near_q, returned[0]).astype(jnp.float32)
        grad_k_sum = grad_k_sum + jnp.where(executes, near_k, returned[1]).astype(jnp.float32)
        grad_v_sum = grad_v_sum + jnp.where(executes, near_v, returned[2]).astype(jnp.float32)
    grad_q = (
        norm_back(q_float, q_inverse, gain_q, grad_q_sum)
        .reshape(tokens_here, -1)
        .astype(jnp.bfloat16)
    )
    grad_k = (
        norm_back(k_float, k_inverse, gain_k, grad_k_sum)
        .reshape(tokens_here, -1)
        .astype(jnp.bfloat16)
    )
    grad_v = grad_v_sum.reshape(tokens_here, -1).astype(jnp.bfloat16)
    local_gain_q = jnp.sum(grad_q_sum * q_float * q_inverse, axis=(0, 1))
    local_gain_k = jnp.sum(grad_k_sum * k_float * k_inverse, axis=(0, 1))
    grad_gain_q, grad_gain_k = lax.psum((local_gain_q, local_gain_k), ("ctx", "head"))
    return (grad_q, grad_k, grad_v, grad_gain_q, grad_gain_k)


def solution(mesh):
    placed = (
        P("ctx", "head"),
        P("ctx", "head"),
        P("ctx", "head"),
        P("ctx", "head"),
        P(),
        P(),
        P("ctx", None),
        P("ctx"),
    )
    return jax.shard_map(
        body,
        mesh=mesh,
        in_specs=placed,
        out_specs=(P("ctx", "head"), P("ctx", "head"), P("ctx", "head"), P(), P()),
        check_vma=False,
    )
```

profile of v0, /device:TPU:1, one launch (start us, length us, event | category | flops | bytes accessed | tf_op | source)
XLA Modules:
  0.0 293.7 jit_solution(8357345326134544632)
XLA Ops:
  1.8 3.9 %collective-permute-start.7 = (bf16[256,5,128]{0,2,1:T(8,128)(2,1)S(1)}, bf16[256,5,128]{0,2,1:T(8,128)(2,1)}, u32[]{:S(2)}, u32[]{:S(2)}) collective-permute-start(bf16[256,5,128]{0,2,1:T(8,128)(2,1)S(1)} %bitcast.136), channel_id=1, source_target_pairs={{0,16},{16,0},{8,24},{24,8},{32,48},{48,32},{40,56},{56,40},{64,80... | collective-permute-start | bytes 983048 | tf_op jit(solution)/shard_map/ppermute | solution.py:22
  10.0 9.2 %collective-permute-start = (bf16[1]{0:T(256)(128)(2,1)}, bf16[1]{0:T(256)(128)(2,1)}, u32[]{:S(2)}, u32[]{:S(2)}) collective-permute-start(bf16[1]{0:T(256)(128)(2,1)} %bitcast.19), channel_id=1, source_target_pairs={{0,8},{8,0},{16,24},{24,16},{32,40},{40,32},{48,56},{56,48},{64,72... | collective-permute-start | bytes 14 | tf_op jit(solution)/shard_map/ppermute | solution.py:22
  23.3 10.2 %collective-permute-start.5 = (bf16[1]{0:T(256)(128)(2,1)}, bf16[1]{0:T(256)(128)(2,1)}, u32[]{:S(2)}, u32[]{:S(2)}) collective-permute-start(bf16[1]{0:T(256)(128)(2,1)} %bitcast.22), channel_id=1, source_target_pairs={{0,16},{16,0},{8,24},{24,8},{32,48},{48,32},{40,56},{56,40},{64,80... | collective-permute-start | bytes 14 | tf_op jit(solution)/shard_map/ppermute | solution.py:22
  33.5 2.8 collective-permute-start.8
  41.3 9.9 %conditional.4 = (f32[5,256]{1,0:T(8,128)}, f32[5,256]{1,0:T(8,128)}, f32[256,5,128]{2,0,1:T(8,128)}, f32[256,5,128]{0,2,1:T(8,128)}) conditional(s32[]{:T(128)} %convert_element_type.181, () %tuple.40, (bf16[256,5,128]{0,2,1:T(8,128)(2,1)S(1)}, bf16[256,5,128]{0,2,1:T(8,128)(2,1)}, bf16[256,5,128]{0,2,1:T(8,128)(2,1)}, ...), branch_computations={%region_5.6_spmd, %region_6.11_spmd} | conditional | flops 339473920 | bytes 13834300 | solution.py:132
  51.2 12.4 %collective-permute-done.8 = bf16[256,5,128]{0,2,1:T(8,128)(2,1)} collective-permute-done((bf16[256,5,128]{0,2,1:T(8,128)(2,1)S(1)}, bf16[256,5,128]{0,2,1:T(8,128)(2,1)}, u32[]{:S(2)}, u32[]{:S(2)}) %collective-permute-start.8) | collective-permute-done | bytes 327712 | tf_op jit(solution)/shard_map/ppermute | solution.py:22
  63.6 7.0 %collective-permute-done.6 = bf16[256,5,128]{0,2,1:T(8,128)(2,1)} collective-permute-done((bf16[256,5,128]{0,2,1:T(8,128)(2,1)S(1)}, bf16[256,5,128]{0,2,1:T(8,128)(2,1)}, u32[]{:S(2)}, u32[]{:S(2)}) %collective-permute-start.6) | collective-permute-done | bytes 327712 | tf_op jit(solution)/shard_map/ppermute | solution.py:22
  70.6 3.0 %conditional.5 = (f32[5,256]{1,0:T(8,128)}, f32[5,256]{1,0:T(8,128)}, f32[256,5,128]{2,0,1:T(8,128)}, f32[256,5,128]{0,2,1:T(8,128)}) conditional(s32[]{:T(128)} %convert_element_type.183, () %tuple.42, (bf16[256,5,128]{0,2,1:T(8,128)(2,1)S(1)}, bf16[256,5,128]{0,2,1:T(8,128)(2,1)}, bf16[256,5,128]{0,2,1:T(8,128)(2,1)}, ...), branch_computations={%region_12.13_spmd, %region_13.18_spmd} | conditional | flops 339473920 | bytes 12523552 | solution.py:132
  73.6 6.3 %collective-permute-start.9 = (f32[5,256]{1,0:T(8,128)}, f32[5,256]{1,0:T(8,128)S(1)}, u32[]{:S(2)}, u32[]{:S(2)}) collective-permute-start(f32[5,256]{1,0:T(8,128)} %get-tuple-element.136), channel_id=1, source_target_pairs={{0,16},{16,0},{8,24},{24,8},{32,48},{48,32},{40,56},{56,40},{64,80... | collective-permute-start | bytes 15368 | tf_op jit(solution)/shard_map/ppermute | solution.py:22
  82.3 3.9 %collective-permute-start.10 = (f32[256,5,128]{0,2,1:T(8,128)}, f32[256,5,128]{0,2,1:T(8,128)}, u32[]{:S(2)}, u32[]{:S(2)}) collective-permute-start(f32[256,5,128]{0,2,1:T(8,128)} %copy.109), channel_id=1, source_target_pairs={{0,8},{8,0},{16,24},{24,16},{32,40},{40,32},{48,56},{56,48},{64,72... | collective-permute-start | bytes 1966088 | tf_op jit(solution)/shard_map/ppermute | solution.py:22
  89.1 2.5 collective-permute-start.16
  91.9 15.5 %collective-permute-done.10 = f32[256,5,128]{0,2,1:T(8,128)} collective-permute-done((f32[256,5,128]{0,2,1:T(8,128)}, f32[256,5,128]{0,2,1:T(8,128)}, u32[]{:S(2)}, u32[]{:S(2)}) %collective-permute-start.10) | collective-permute-done | bytes 655392 | tf_op jit(solution)/shard_map/ppermute | solution.py:22
  107.3 8.8 %collective-permute-done.11 = f32[256,5,128]{0,2,1:T(8,128)S(1)} collective-permute-done((f32[256,5,128]{0,2,1:T(8,128)}, f32[256,5,128]{0,2,1:T(8,128)S(1)}, u32[]{:S(2)}, u32[]{:S(2)}) %collective-permute-start.11) | collective-permute-done | bytes 655392 | tf_op jit(solution)/shard_map/ppermute | solution.py:22
  120.7 21.8 %conditional.6 = (bf16[256,5,128]{2,0,1:T(8,128)(2,1)}, bf16[256,5,128]{2,0,1:T(8,128)(2,1)}, bf16[256,5,128]{2,0,1:T(8,128)(2,1)}, bf16[256,5,128]{0,2,1:T(8,12...) conditional(s32[]{:T(128)} %convert_element_type.181, () %tuple.44, ...), branch_computations={%region_20.21_spmd, %region_21.22_spmd} | conditional | flops 844431360 | bytes 24268904 | solution.py:167
  122.1 2.2 fusion.13
  128.3 2.2 fusion.17
  144.4 3.9 %conditional.7 = (bf16[256,5,128]{2,0,1:T(8,128)(2,1)}, bf16[256,5,128]{2,0,1:T(8,128)(2,1)}, bf16[256,5,128]{2,0,1:T(8,128)(2,1)}, bf16[256,5,128]{0,2,1:T(8,12...) conditional(s32[]{:T(128)} %convert_element_type.183, () %tuple.46, ...), branch_computations={%region_22.23_spmd, %region_23.24_spmd} | conditional | flops 844431360 | bytes 22958156 | solution.py:167
  150.2 20.1 %collective-permute-start.21 = (bf16[256,5,128]{0,2,1:T(8,128)(2,1)}, bf16[256,5,128]{0,2,1:T(8,128)(2,1)}, u32[]{:S(2)}, u32[]{:S(2)}) collective-permute-start(bf16[256,5,128]{0,2,1:T(8,128)(2,1)} %copy.138), channel_id=1, source_target_pairs={{0,16},{16,0},{8,24},{24,8},{32,48},{48,32},{40,56},{56,40},{64,80... | collective-permute-start | bytes 983048 | tf_op jit(solution)/shard_map/ppermute | solution.py:22
  170.4 2.3 convolution_bitcast_fusion.6
  183.9 2.4 collective-permute-start.19
  186.2 2.6 multiply_reduce_fusion
  188.8 12.3 %collective-permute-done.23 = bf16[256,5,128]{0,2,1:T(8,128)(2,1)S(1)} collective-permute-done((bf16[256,5,128]{0,2,1:T(8,128)(2,1)}, bf16[256,5,128]{0,2,1:T(8,128)(2,1)S(1)}, u32[]{:S(2)}, u32[]{:S(2)}) %collective-permute-start.23) | collective-permute-done | bytes 327712 | tf_op jit(solution)/shard_map/ppermute | solution.py:22
  206.9 5.7 %collective-permute-done.19 = bf16[256,5,128]{0,2,1:T(8,128)(2,1)} collective-permute-done((bf16[256,5,128]{0,2,1:T(8,128)(2,1)}, bf16[256,5,128]{0,2,1:T(8,128)(2,1)}, u32[]{:S(2)}, u32[]{:S(2)}) %collective-permute-start.19) | collective-permute-done | bytes 327712 | tf_op jit(solution)/shard_map/ppermute | solution.py:22
  215.3 78.4 %all-reduce = (f32[128]{0:T(128)}, f32[128]{0:T(128)}) all-reduce(f32[128]{0:T(128)S(1)} %get-tuple-element.249, f32[128]{0:T(128)S(1)} %get-tuple-element.247), channel_id=1, replica_groups=mesh['ctx'=32,'head'=8] {'ctx','head'}, use_global_device_ids=true, to_apply=%region_27.28 | all-reduce | flops 256 | bytes 2048 | tf_op jit(solution)/shard_map/psum | solution.py:188
  (128 shorter events, 78.6 us)
Async XLA Ops:
  1.8 49.4 %collective-permute-start.7 = (bf16[256,5,128]{0,2,1:T(8,128)(2,1)S(1)}, bf16[256,5,128]{0,2,1:T(8,128)(2,1)}, u32[]{:S(2)}, u32[]{:S(2)}) collective-permute-start(bf16[256,5,128]{0,2,1:T(8,128)(2,1)S(1)} %bitcast.136), channel_id=1, source_target_pairs={{0,16},{16,0},{8,24},{24,8},{32,48},{48,32},{40,56},{56,40},{64,80... | collective-permute-start | bytes 983048 | tf_op jit(solution)/shard_map/ppermute | solution.py:22
  5.7 30.6 %collective-permute-start.2 = (bf16[256,5,128]{0,2,1:T(8,128)(2,1)S(1)}, bf16[256,5,128]{0,2,1:T(8,128)(2,1)S(1)}, u32[]{:S(2)}, u32[]{:S(2)}) collective-permute-start(bf16[256,5,128]{0,2,1:T(8,128)(2,1)S(1)} %bitcast.137), channel_id=1, source_target_pairs={{0,8},{8,0},{16,24},{24,16},{32,40},{40,32},{48,56},{56,48},{64,72... | collective-permute-start | bytes 983048 | tf_op jit(solution)/shard_map/ppermute | solution.py:22
  10.0 13.3 %collective-permute-start = (bf16[1]{0:T(256)(128)(2,1)}, bf16[1]{0:T(256)(128)(2,1)}, u32[]{:S(2)}, u32[]{:S(2)}) collective-permute-start(bf16[1]{0:T(256)(128)(2,1)} %bitcast.19), channel_id=1, source_target_pairs={{0,8},{8,0},{16,24},{24,16},{32,40},{40,32},{48,56},{56,48},{64,72... | collective-permute-start | bytes 14 | tf_op jit(solution)/shard_map/ppermute | solution.py:22
  20.6 18.3 %collective-permute-start.3 = (bf16[256,5,128]{0,2,1:T(8,128)(2,1)S(1)}, bf16[256,5,128]{0,2,1:T(8,128)(2,1)}, u32[]{:S(2)}, u32[]{:S(2)}) collective-permute-start(bf16[256,5,128]{0,2,1:T(8,128)(2,1)S(1)} %multiply_convert_fusion), channel_id=1, source_target_pairs={{0,8},{8,0},{16,24},{24,16},{32,40},{40,32},{48,56},{56,48},{64,72... | collective-permute-start | bytes 983048 | tf_op jit(solution)/shard_map/ppermute | solution.py:22
  21.2 19.4 %collective-permute-start.1 = (bf16[256,5,128]{0,2,1:T(8,128)(2,1)S(1)}, bf16[256,5,128]{0,2,1:T(8,128)(2,1)}, u32[]{:S(2)}, u32[]{:S(2)}) collective-permute-start(bf16[256,5,128]{0,2,1:T(8,128)(2,1)S(1)} %multiply_convert_fusion.1), channel_id=1, source_target_pairs={{0,8},{8,0},{16,24},{24,16},{32,40},{40,32},{48,56},{56,48},{64,72... | collective-permute-start | bytes 983048 | tf_op jit(solution)/shard_map/ppermute | solution.py:22
  23.3 10.2 %collective-permute-start.5 = (bf16[1]{0:T(256)(128)(2,1)}, bf16[1]{0:T(256)(128)(2,1)}, u32[]{:S(2)}, u32[]{:S(2)}) collective-permute-start(bf16[1]{0:T(256)(128)(2,1)} %bitcast.22), channel_id=1, source_target_pairs={{0,16},{16,0},{8,24},{24,8},{32,48},{48,32},{40,56},{56,40},{64,80... | collective-permute-start | bytes 14 | tf_op jit(solution)/shard_map/ppermute | solution.py:22
  33.5 30.1 %collective-permute-start.8 = (bf16[256,5,128]{0,2,1:T(8,128)(2,1)S(1)}, bf16[256,5,128]{0,2,1:T(8,128)(2,1)}, u32[]{:S(2)}, u32[]{:S(2)}) collective-permute-start(bf16[256,5,128]{0,2,1:T(8,128)(2,1)S(1)} %multiply_convert_fusion), channel_id=1, source_target_pairs={{0,16},{16,0},{8,24},{24,8},{32,48},{48,32},{40,56},{56,40},{64,80... | collective-permute-start | bytes 983048 | tf_op jit(solution)/shard_map/ppermute | solution.py:22
  36.3 34.3 %collective-permute-start.6 = (bf16[256,5,128]{0,2,1:T(8,128)(2,1)S(1)}, bf16[256,5,128]{0,2,1:T(8,128)(2,1)}, u32[]{:S(2)}, u32[]{:S(2)}) collective-permute-start(bf16[256,5,128]{0,2,1:T(8,128)(2,1)S(1)} %multiply_convert_fusion.1), channel_id=1, source_target_pairs={{0,16},{16,0},{8,24},{24,8},{32,48},{48,32},{40,56},{56,40},{64,80... | collective-permute-start | bytes 983048 | tf_op jit(solution)/shard_map/ppermute | solution.py:22
  38.9 105.4 %collective-permute-start.17 = (bf16[256,5,128]{0,2,1:T(8,128)(2,1)S(1)}, bf16[256,5,128]{0,2,1:T(8,128)(2,1)}, u32[]{:S(2)}, u32[]{:S(2)}) collective-permute-start(bf16[256,5,128]{0,2,1:T(8,128)(2,1)S(1)} %bitcast.129), channel_id=1, source_target_pairs={{0,16},{16,0},{8,24},{24,8},{32,48},{48,32},{40,56},{56,40},{64,80... | collective-permute-start | bytes 983048 | tf_op jit(solution)/shard_map/ppermute | solution.py:22
  40.6 77.0 %collective-permute-start.13 = (bf16[256,5,128]{0,2,1:T(8,128)(2,1)S(1)}, bf16[256,5,128]{0,2,1:T(8,128)(2,1)}, u32[]{:S(2)}, u32[]{:S(2)}) collective-permute-start(bf16[256,5,128]{0,2,1:T(8,128)(2,1)S(1)} %bitcast.130), channel_id=1, source_target_pairs={{0,8},{8,0},{16,24},{24,16},{32,40},{40,32},{48,56},{56,48},{64,72... | collective-permute-start | bytes 983048 | tf_op jit(solution)/shard_map/ppermute | solution.py:22
  51.2 37.1 %collective-permute-start.4 = (f32[5,256]{1,0:T(8,128)}, f32[5,256]{1,0:T(8,128)S(1)}, u32[]{:S(2)}, u32[]{:S(2)}) collective-permute-start(f32[5,256]{1,0:T(8,128)} %get-tuple-element.134), channel_id=1, source_target_pairs={{0,8},{8,0},{16,24},{24,16},{32,40},{40,32},{48,56},{56,48},{64,72... | collective-permute-start | bytes 15368 | tf_op jit(solution)/shard_map/ppermute | solution.py:22
  73.6 14.7 %collective-permute-start.9 = (f32[5,256]{1,0:T(8,128)}, f32[5,256]{1,0:T(8,128)S(1)}, u32[]{:S(2)}, u32[]{:S(2)}) collective-permute-start(f32[5,256]{1,0:T(8,128)} %get-tuple-element.136), channel_id=1, source_target_pairs={{0,16},{16,0},{8,24},{24,8},{32,48},{48,32},{40,56},{56,40},{64,80... | collective-permute-start | bytes 15368 | tf_op jit(solution)/shard_map/ppermute | solution.py:22
  82.3 25.1 %collective-permute-start.10 = (f32[256,5,128]{0,2,1:T(8,128)}, f32[256,5,128]{0,2,1:T(8,128)}, u32[]{:S(2)}, u32[]{:S(2)}) collective-permute-start(f32[256,5,128]{0,2,1:T(8,128)} %copy.109), channel_id=1, source_target_pairs={{0,8},{8,0},{16,24},{24,16},{32,40},{40,32},{48,56},{56,48},{64,72... | collective-permute-start | bytes 1966088 | tf_op jit(solution)/shard_map/ppermute | solution.py:22
  88.3 27.9 %collective-permute-start.11 = (f32[256,5,128]{0,2,1:T(8,128)}, f32[256,5,128]{0,2,1:T(8,128)S(1)}, u32[]{:S(2)}, u32[]{:S(2)}) collective-permute-start(f32[256,5,128]{0,2,1:T(8,128)} %copy.111), channel_id=1, source_target_pairs={{0,16},{16,0},{8,24},{24,8},{32,48},{48,32},{40,56},{56,40},{64,80... | collective-permute-start | bytes 1966088 | tf_op jit(solution)/shard_map/ppermute | solution.py:22
  89.1 55.3 %collective-permute-start.16 = (f32[5,256]{1,0:T(8,128)S(1)}, f32[5,256]{1,0:T(8,128)S(1)}, u32[]{:S(2)}, u32[]{:S(2)}) collective-permute-start(f32[5,256]{1,0:T(8,128)S(1)} %get-tuple-element.252), channel_id=1, source_target_pairs={{0,16},{16,0},{8,24},{24,8},{32,48},{48,32},{40,56},{56,40},{64,80... | collective-permute-start | bytes 15368 | tf_op jit(solution)/shard_map/ppermute | solution.py:22
  107.3 11.7 %collective-permute-start.12 = (f32[5,256]{1,0:T(8,128)S(1)}, f32[5,256]{1,0:T(8,128)S(1)}, u32[]{:S(2)}, u32[]{:S(2)}) collective-permute-start(f32[5,256]{1,0:T(8,128)S(1)} %get-tuple-element.252), channel_id=1, source_target_pairs={{0,8},{8,0},{16,24},{24,16},{32,40},{40,32},{48,56},{56,48},{64,72... | collective-permute-start | bytes 15368 | tf_op jit(solution)/shard_map/ppermute | solution.py:22
  117.5 26.8 %collective-permute-start.18 = (f32[5,256]{1,0:T(8,128)S(1)}, f32[5,256]{1,0:T(8,128)S(1)}, u32[]{:S(2)}, u32[]{:S(2)}) collective-permute-start(f32[5,256]{1,0:T(8,128)S(1)} %bitcast.155), channel_id=1, source_target_pairs={{0,16},{16,0},{8,24},{24,8},{32,48},{48,32},{40,56},{56,40},{64,80... | collective-permute-start | bytes 15368 | tf_op jit(solution)/shard_map/ppermute | solution.py:22
  117.6 3.1 %collective-permute-start.14 = (f32[5,256]{1,0:T(8,128)S(1)}, f32[5,256]{1,0:T(8,128)S(1)}, u32[]{:S(2)}, u32[]{:S(2)}) collective-permute-start(f32[5,256]{1,0:T(8,128)S(1)} %bitcast.156), channel_id=1, source_target_pairs={{0,8},{8,0},{16,24},{24,16},{32,40},{40,32},{48,56},{56,48},{64,72... | collective-permute-start | bytes 15368 | tf_op jit(solution)/shard_map/ppermute | solution.py:22
  144.3 39.5 %collective-permute-start.20 = (bf16[256,5,128]{0,2,1:T(8,128)(2,1)}, bf16[256,5,128]{0,2,1:T(8,128)(2,1)}, u32[]{:S(2)}, u32[]{:S(2)}) collective-permute-start(bf16[256,5,128]{0,2,1:T(8,128)(2,1)} %copy.136), channel_id=1, source_target_pairs={{0,8},{8,0},{16,24},{24,16},{32,40},{40,32},{48,56},{56,48},{64,72... | collective-permute-start | bytes 983048 | tf_op jit(solution)/shard_map/ppermute | solution.py:22
  150.2 36.0 %collective-permute-start.21 = (bf16[256,5,128]{0,2,1:T(8,128)(2,1)}, bf16[256,5,128]{0,2,1:T(8,128)(2,1)}, u32[]{:S(2)}, u32[]{:S(2)}) collective-permute-start(bf16[256,5,128]{0,2,1:T(8,128)(2,1)} %copy.138), channel_id=1, source_target_pairs={{0,16},{16,0},{8,24},{24,8},{32,48},{48,32},{40,56},{56,40},{64,80... | collective-permute-start | bytes 983048 | tf_op jit(solution)/shard_map/ppermute | solution.py:22
  174.6 14.3 %collective-permute-start.22 = (bf16[256,5,128]{0,2,1:T(8,128)(2,1)}, bf16[256,5,128]{0,2,1:T(8,128)(2,1)S(1)}, u32[]{:S(2)}, u32[]{:S(2)}) collective-permute-start(bf16[256,5,128]{0,2,1:T(8,128)(2,1)} %copy.141), channel_id=1, source_target_pairs={{0,8},{8,0},{16,24},{24,16},{32,40},{40,32},{48,56},{56,48},{64,72... | collective-permute-start | bytes 983048 | tf_op jit(solution)/shard_map/ppermute | solution.py:22
  177.9 23.3 %collective-permute-start.23 = (bf16[256,5,128]{0,2,1:T(8,128)(2,1)}, bf16[256,5,128]{0,2,1:T(8,128)(2,1)S(1)}, u32[]{:S(2)}, u32[]{:S(2)}) collective-permute-start(bf16[256,5,128]{0,2,1:T(8,128)(2,1)} %copy.143), channel_id=1, source_target_pairs={{0,16},{16,0},{8,24},{24,8},{32,48},{48,32},{40,56},{56,40},{64,80... | collective-permute-start | bytes 983048 | tf_op jit(solution)/shard_map/ppermute | solution.py:22
  182.0 24.9 %collective-permute-start.15 = (bf16[256,5,128]{0,2,1:T(8,128)(2,1)}, bf16[256,5,128]{0,2,1:T(8,128)(2,1)}, u32[]{:S(2)}, u32[]{:S(2)}) collective-permute-start(bf16[256,5,128]{0,2,1:T(8,128)(2,1)} %copy.123), channel_id=1, source_target_pairs={{0,8},{8,0},{16,24},{24,16},{32,40},{40,32},{48,56},{56,48},{64,72... | collective-permute-start | bytes 983048 | tf_op jit(solution)/shard_map/ppermute | solution.py:22
  183.9 28.8 %collective-permute-start.19 = (bf16[256,5,128]{0,2,1:T(8,128)(2,1)}, bf16[256,5,128]{0,2,1:T(8,128)(2,1)}, u32[]{:S(2)}, u32[]{:S(2)}) collective-permute-start(bf16[256,5,128]{0,2,1:T(8,128)(2,1)} %copy.133), channel_id=1, source_target_pairs={{0,16},{16,0},{8,24},{24,8},{32,48},{48,32},{40,56},{56,40},{64,80... | collective-permute-start | bytes 983048 | tf_op jit(solution)/shard_map/ppermute | solution.py:22
  (15 other events, 135.6 us)
where the time goes:
time: 296 us; the launch traced here: 294 us
  blocking collectives  78.4 us (26%)
  starting transfers between devices  68.6 us (23%)
  waiting for transfers between devices  63.4 us (21%)
  local copies, waits for them, and re-layouts  37.2 us (13%)
  matrix products  30.9 us (10%)
  other arithmetic  10.9 us (4%)
  between operations  4.14 us (1%)
    psum x1, blocking collectives, body(): lax.psum((local_gain_q, local_gain_k), ('ctx', 'head'))  78.4 us
    ppermute x24, starting transfers between devices, from_partner(): return lax.ppermute(block, axis, route)  68.6 us
    ppermute x24, waiting for transfers between devices, from_partner(): return lax.ppermute(block, axis, route)  63.4 us
    cond x9, local copies, waits for them, and re-layouts, body(): lax.cond(run_flags[bit_index], backward_both, backward_none)  17 us
    cond x3, local copies, waits for them, and re-layouts, body(): lax.cond(runs_here, forward_both, forward_none)  6.51 us
    dot_general x3, matrix products, both_sides(): jnp.einsum('hts,shd->thd', grad_score, key_rows, preferred_element_type=j...  6.46 us
  transfers between devices with their start and end apart: 24, of which 7 were waited for; matrix products, arithmetic and copies ran while one was open for 25% of the time, Pallas kernels for 0%

commit v1 on v0

v1 whole, which is shorter than its diff:
```python
import math

import jax
import jax.numpy as jnp
from jax import lax
from jax.experimental import pallas as pl
from jax.experimental.pallas import tpu as pltpu
from jax.sharding import PartitionSpec as P

HEAD_DIM = 128
BITS = 2
ROWS = 256
HEADS = 5
FLOOR_LOG = -1e30
FACTOR = 1.0 / math.sqrt(HEAD_DIM)
LOG2E = 1.0 / math.log(2.0)
HEAD_DEVS = 8
Y_DEVS = 4
Z_DEVS = 8
PEERS = (HEAD_DEVS - 1) + (Y_DEVS - 1) + (Z_DEVS - 1)
MESH = pl.DeviceIdType.MESH
NT = (((1,), (1,)), ((), ()))
NN = (((1,), (0,)), ((), ()))
TN = (((0,), (0,)), ((), ()))


def mm(a, b, dims):
    return lax.dot_general(a, b, dims, preferred_element_type=jnp.float32)


def kernel(
    q_hbm, k_hbm, v_hbm, g_hbm, gain_q_ref, gain_k_ref, blocks_ref, count_ref,
    oq_hbm, ok_hbm, ov_hbm, ogain_q_ref, ogain_k_ref,
    raw_q, raw_k, qn, kn, vn, gn, rq, rg,
    q_hat, q_inv, k_hat, k_inv, prob, dprob, stat_own, stat_out, stat_in,
    fin_own, fin_out, fin_in, dq_own, dq_out, dq_in, oq, ok, ov, acc,
    sum_a, sum_b, sum_c,
    load_sem, store_sem, qs, qr, gs, gr, ss, sr, fs, fr, ds, dr, as_, ar,
):
    place = lax.axis_index("ctx")
    column = lax.axis_index("head")
    z = lax.rem(place, Z_DEVS)
    y = lax.div(place, Z_DEVS)
    partners = [jnp.bitwise_xor(place, 1 << i) for i in range(BITS)]
    lower = [jnp.bitwise_and(place, 1 << i) == 0 for i in range(BITS)]

    head_peers = [{"head": lax.rem(column + r, HEAD_DEVS)} for r in range(1, HEAD_DEVS)]
    y_peers = [{"ctx": lax.rem(y + r, Y_DEVS) * Z_DEVS + z} for r in range(1, Y_DEVS)]
    z_peers = [{"ctx": y * Z_DEVS + lax.rem(z + r, Z_DEVS)} for r in range(1, Z_DEVS)]

    barrier = pltpu.get_barrier_semaphore()
    for peer in z_peers + y_peers + head_peers:
        pl.semaphore_signal(barrier, 1, device_id=peer, device_id_type=MESH)

    def load(src, dst, slot, h):
        return pltpu.make_async_copy(
            src.at[:, h * HEAD_DIM : (h + 1) * HEAD_DIM], dst.at[h], load_sem.at[slot, h]
        )

    sources = ((g_hbm, gn), (q_hbm, raw_q), (k_hbm, raw_k), (v_hbm, vn))
    for slot, (src, dst) in enumerate(sources):
        for h in range(HEADS):
            load(src, dst, slot, h).start()

    def remote(src, dst, send, recv, peer):
        return pltpu.make_async_remote_copy(
            src_ref=src, dst_ref=dst, send_sem=send, recv_sem=recv,
            device_id=peer, device_id_type=MESH,
        )

    def q_copy(h, i):
        return remote(qn.at[h], rq.at[i, h], qs.at[i, h], qr.at[i, h], {"ctx": partners[i]})

    def g_copy(h, i):
        return remote(gn.at[h], rg.at[i, h], gs.at[i, h], gr.at[i, h], {"ctx": partners[i]})

    def s_copy(h, i):
        return remote(stat_out.at[i, h], stat_in.at[i, h], ss.at[i, h], sr.at[i, h], {"ctx": partners[i]})

    def f_copy(h, i):
        return remote(fin_out.at[i, h], fin_in.at[i, h], fs.at[i, h], fr.at[i, h], {"ctx": partners[i]})

    def d_copy(h, i):
        return remote(dq_out.at[i, h], dq_in.at[i, h], ds.at[i, h], dr.at[i, h], {"ctx": partners[i]})

    listed = []
    for i in range(BITS):
        hit = jnp.float32(0.0)
        for slot in range(BITS):
            live = (blocks_ref[0, slot] == partners[i]) & (slot < count_ref[0])
            hit = jnp.where(live, 1.0, hit)
        listed.append(hit)
    off = [jnp.where(lower[i], 1.0 - listed[i], 0.0) for i in range(BITS)]

    gain_q = gain_q_ref[...]
    gain_k = gain_k_ref[...]

    def norm(raw, gain, hat, inv, normed, h):
        x = raw[h].astype(jnp.float32)
        inverse = lax.rsqrt(jnp.mean(x * x, axis=1, keepdims=True) + 1e-06)
        x_hat = x * inverse
        hat[h] = x_hat
        inv[h] = jnp.broadcast_to(inverse, x.shape)
        normed[h] = (x_hat * gain).astype(jnp.bfloat16)

    for h in range(HEADS):
        load(q_hbm, raw_q, 1, h).wait()
        load(g_hbm, gn, 0, h).wait()
        norm(raw_q, gain_q, q_hat, q_inv, qn, h)
        if h == 0:
            pl.semaphore_wait(barrier, PEERS)
        for i in (1, 0):
            g_copy(h, i).start()
            q_copy(h, i).start()
    for h in range(HEADS):
        load(k_hbm, raw_k, 2, h).wait()
        load(v_hbm, vn, 3, h).wait()
        norm(raw_k, gain_k, k_hat, k_inv, kn, h)
    acc[...] = jnp.zeros_like(acc)

    def forward(h, slot, query, grad):
        scores = mm(kn[h], query, NT)
        largest = jnp.max(scores, axis=0, keepdims=True)
        e = jnp.exp2((scores - largest) * (FACTOR * LOG2E))
        total = jnp.sum(e, axis=0, keepdims=True)
        p = e * (1.0 / total)
        dp = mm(vn[h], grad, NT)
        prob[slot, h] = p
        dprob[slot, h] = dp
        dot = jnp.sum(p.astype(jnp.bfloat16).astype(jnp.float32) * dp, axis=0, keepdims=True)
        return largest * FACTOR + jnp.log(total), dot

    def far_forward(h):
        for i in (0, 1):
            g_copy(h, i).wait_recv()
            q_copy(h, i).wait_recv()
            log, dot = forward(h, i + 1, rq[i, h], rg[i, h])
            stat_out[i, h, 0:1] = jnp.where(off[i] > 0.5, FLOOR_LOG, log)
            stat_out[i, h, 1:2] = dot
            s_copy(h, i).start()

    def near_forward(h):
        log, dot = forward(h, 0, qn[h], gn[h])
        stat_own[h, 0:1] = log
        stat_own[h, 1:2] = dot

    def combine(h):
        logs = [stat_own[h, 0:1]]
        dots = [stat_own[h, 1:2]]
        for i in range(BITS):
            s_copy(h, i).wait_recv()
            logs.append(jnp.where(off[i] > 0.5, FLOOR_LOG, stat_in[i, h, 0:1]))
            dots.append(stat_in[i, h, 1:2])
        top = jnp.maximum(jnp.maximum(logs[0], logs[1]), logs[2])
        parts = [jnp.exp(log - top) for log in logs]
        inverse = 1.0 / (parts[0] + parts[1] + parts[2])
        shares = [part * inverse for part in parts]
        row_dot = shares[0] * dots[0] + shares[1] * dots[1] + shares[2] * dots[2]
        for i in range(BITS):
            fin_out[i, h, 0:1] = shares[i + 1]
            fin_out[i, h, 1:2] = row_dot
            f_copy(h, i).start()
        fin_own[h, 0:1] = shares[0]
        fin_own[h, 1:2] = row_dot

    def one_back(h, slot, query, grad, share, row_dot):
        w = prob[slot, h] * share
        ds_t = (w * (dprob[slot, h] - row_dot) * FACTOR).astype(jnp.bfloat16)
        dv = mm(w.astype(jnp.bfloat16), grad, NN)
        dk = mm(ds_t, query, NN)
        dq = mm(ds_t, kn[h], TN)
        return dq, dk, dv

    def norm_back(hat, inv, gain, grad):
        gg = grad * gain
        inner = jnp.mean(hat * gg, axis=1, keepdims=True)
        return (inv * (gg - hat * inner)).astype(jnp.bfloat16)

    def fold(a):
        return jnp.sum(a.reshape(ROWS // 8, 8, HEAD_DIM), axis=0)

    def columns(h):
        return pl.ds(pl.multiple_of(h * HEAD_DIM, HEAD_DIM), HEAD_DIM)

    def store(src, dst, slot, h):
        return pltpu.make_async_copy(src.at[h], dst.at[:, columns(h)], store_sem.at[slot, h])

    def backward(h):
        for i in range(BITS):
            f_copy(h, i).wait_recv()
            dq, dk, dv = one_back(
                h, i + 1, rq[i, h], rg[i, h], fin_in[i, h, 0:1], fin_in[i, h, 1:2]
            )
            dq_out[i, h] = dq.astype(jnp.bfloat16)
            d_copy(h, i).start()
            acc[1] += fold(dq * rq[i, h].astype(jnp.float32))
            if i == 0:
                gk, gv = dk, dv
            else:
                gk, gv = gk + dk, gv + dv
        dq, dk, dv = one_back(h, 0, qn[h], gn[h], fin_own[h, 0:1], fin_own[h, 1:2])
        gk, gv = gk + dk, gv + dv
        dq_own[h] = dq
        acc[0] += fold(dq * q_hat[h])
        acc[2] += fold(gk * k_hat[h])
        ov[h] = gv.astype(jnp.bfloat16)
        store(ov, ov_hbm, 2, h).start()
        ok[h] = norm_back(k_hat[h], k_inv[h], gain_k, gk)
        store(ok, ok_hbm, 1, h).start()

    def step(h, carry):
        @pl.when(h < HEADS)
        def _():
            far_forward(h)
            near_forward(h)
            combine(h)

        @pl.when(h > 0)
        def _():
            backward(h - 1)

        return carry

    lax.fori_loop(0, HEADS + 1, step, 0)

    def finish(h):
        for i in range(BITS):
            d_copy(h, i).wait_recv()
        gq = dq_own[h] + dq_in[0, h].astype(jnp.float32) + dq_in[1, h].astype(jnp.float32)
        oq[h] = norm_back(q_hat[h], q_inv[h], gain_q, gq)
        store(oq, oq_hbm, 0, h).start()

    def share_copies(buffer, index, peers, base):
        return [
            remote(buffer.at[index], buffer.at[index], as_.at[base + r], ar.at[base + r], peer)
            for r, peer in enumerate(peers)
        ]

    copies_a = share_copies(sum_a, column, head_peers, 0)
    copies_b = share_copies(sum_b, y, y_peers, HEAD_DEVS - 1)
    copies_c = share_copies(sum_c, z, z_peers, HEAD_DEVS + Y_DEVS - 2)

    part_q = jnp.sum(acc[0], axis=0, keepdims=True) + jnp.sum(acc[1], axis=0, keepdims=True) / gain_q
    sum_a[column, 0:1] = part_q
    sum_a[column, 1:2] = jnp.sum(acc[2], axis=0, keepdims=True)
    for c in copies_a:
        c.start()
    finish(0)
    finish(1)
    for c in copies_a:
        c.wait_recv()
    sum_b[y] = jnp.sum(sum_a[...], axis=0)
    for c in copies_b:
        c.start()
    finish(2)
    for c in copies_b:
        c.wait_recv()
    sum_c[z] = jnp.sum(sum_b[...], axis=0)
    for c in copies_c:
        c.start()
    finish(3)
    finish(4)
    for c in copies_c:
        c.wait_recv()
    total = jnp.sum(sum_c[...], axis=0)
    ogain_q_ref[...] = total[0:1]
    ogain_k_ref[...] = total[1:2]

    for c in copies_a + copies_b + copies_c:
        c.wait_send()
    for h in range(HEADS):
        for i in range(BITS):
            q_copy(h, i).wait_send()
            g_copy(h, i).wait_send()
            s_copy(h, i).wait_send()
            f_copy(h, i).wait_send()
            d_copy(h, i).wait_send()
        for slot, (src, dst) in enumerate(((oq, oq_hbm), (ok, ok_hbm), (ov, ov_hbm))):
            store(src, dst, slot, h).wait()


def body(q_raw, k_raw, values, grad_out, gain_q, gain_k, pair_blocks, pair_count):
    def vmem(*shape, dtype=jnp.float32):
        return pltpu.VMEM(shape, dtype)

    low = jnp.bfloat16
    tile = (HEADS, ROWS, HEAD_DIM)
    square = (BITS + 1, HEADS, ROWS, ROWS)
    wide = jax.ShapeDtypeStruct((ROWS, HEADS * HEAD_DIM), low)
    narrow = jax.ShapeDtypeStruct((1, HEAD_DIM), jnp.float32)
    any_space = pl.BlockSpec(memory_space=pl.ANY)
    in_vmem = pl.BlockSpec(memory_space=pltpu.VMEM)
    in_smem = pl.BlockSpec(memory_space=pltpu.SMEM)
    pair = pltpu.SemaphoreType.DMA((BITS, HEADS))
    grad_q, grad_k, grad_v, sum_q, sum_k = pl.pallas_call(
        kernel,
        out_shape=(wide, wide, wide, narrow, narrow),
        in_specs=[any_space] * 4 + [in_vmem] * 2 + [in_smem] * 2,
        out_specs=(any_space, any_space, any_space, in_vmem, in_vmem),
        scratch_shapes=[
            vmem(*tile, dtype=low), vmem(*tile, dtype=low),
            vmem(*tile, dtype=low), vmem(*tile, dtype=low), vmem(*tile, dtype=low), vmem(*tile, dtype=low),
            vmem(BITS, *tile, dtype=low), vmem(BITS, *tile, dtype=low),
            vmem(*tile), vmem(*tile), vmem(*tile), vmem(*tile),
            vmem(*square), vmem(*square),
            vmem(HEADS, 2, ROWS), vmem(BITS, HEADS, 2, ROWS), vmem(BITS, HEADS, 2, ROWS),
            vmem(HEADS, 2, ROWS), vmem(BITS, HEADS, 2, ROWS), vmem(BITS, HEADS, 2, ROWS),
            vmem(*tile), vmem(BITS, *tile, dtype=low), vmem(BITS, *tile, dtype=low),
            vmem(*tile, dtype=low), vmem(*tile, dtype=low), vmem(*tile, dtype=low),
            vmem(3, 8, HEAD_DIM),
            vmem(HEAD_DEVS, 2, HEAD_DIM), vmem(Y_DEVS, 2, HEAD_DIM), vmem(Z_DEVS, 2, HEAD_DIM),
            pltpu.SemaphoreType.DMA((4, HEADS)), pltpu.SemaphoreType.DMA((3, HEADS)),
            pair, pair, pair, pair, pair, pair, pair, pair, pair, pair,
            pltpu.SemaphoreType.DMA((PEERS,)), pltpu.SemaphoreType.DMA((PEERS,)),
        ],
        compiler_params=pltpu.CompilerParams(
            collective_id=0, has_side_effects=True, vmem_limit_bytes=40 * 1024 * 1024
        ),
        cost_estimate=pl.CostEstimate(
            flops=2 * 5 * 15 * ROWS * ROWS * HEAD_DIM,
            bytes_accessed=7 * ROWS * HEADS * HEAD_DIM * 2,
            transcendentals=15 * ROWS * ROWS,
        ),
    )(
        q_raw, k_raw, values, grad_out,
        gain_q.reshape(1, HEAD_DIM), gain_k.reshape(1, HEAD_DIM), pair_blocks, pair_count,
    )
    return grad_q, grad_k, grad_v, sum_q.reshape(HEAD_DIM), sum_k.reshape(HEAD_DIM)


def solution(mesh):
    placed = (
        P("ctx", "head"),
        P("ctx", "head"),
        P("ctx", "head"),
        P("ctx", "head"),
        P(),
        P(),
        P("ctx", None),
        P("ctx"),
    )
    return jax.shard_map(
        body,
        mesh=mesh,
        in_specs=placed,
        out_specs=(P("ctx", "head"), P("ctx", "head"), P("ctx", "head"), P(), P()),
        check_vma=False,
    )
```

time: 296 us -> 86.1 us (0.29)
  blocking collectives: 78.4 us -> 0 us
  Pallas kernels: 0 us -> 76.8 us
  starting transfers between devices: 68.6 us -> 0 us
  waiting for transfers between devices: 63.4 us -> 0 us
  matrix products: 30.9 us -> 0 us
  local copies, waits for them, and re-layouts: 37.2 us -> 7.75 us
  other arithmetic: 10.9 us -> 0 us
    psum x1 -> x0, blocking collectives: 78.4 us -> none  [body(): lax.psum((local_gain_q, local_gain_k), ('ctx', 'head'))]
    pallas_call x0 -> x1, Pallas kernels: none -> 76.8 us  [body(): pl.pallas_call(kernel, out_shape=(wide, wide, wide, narrow, narrow), in_s...]
    ppermute x24 -> x0, starting transfers between devices: 68.6 us -> none  [from_partner(): return lax.ppermute(block, axis, route)]
    ppermute x24 -> x0, waiting for transfers between devices: 63.4 us -> none  [from_partner(): return lax.ppermute(block, axis, route)]
    dot_general x20 -> x0, matrix products: 30.9 us -> none  [the longest x3 6.46 us: both_sides(): jnp.einsum('hts,shd->thd', grad_score, key_rows, preferred_element_type=j...]
    cond x18 -> x0, local copies, waits for them, and re-layouts: 23.5 us -> none  [the longest x9 17 us: body(): lax.cond(run_flags[bit_index], backward_both, backward_none)]
    broadcast_in_dim x10 -> x0, local copies, waits for them, and re-layouts: 6.81 us -> none  [the longest x6 3.84 us: body(): empty_grad = jnp.zeros((tokens_here, heads_here, HEAD_DIM), jnp.bfloat16)]
    reduce_sum x9 -> x0, other arithmetic: 6.07 us -> none  [the longest x1 2.61 us: body(): local_gain_k = jnp.sum(grad_k_sum * k_float * k_inverse, axis=(0, 1))]
  transfers between devices with their start and end apart: 24 -> 0, of which waited for: 7 -> 0; matrix products, arithmetic and copies ran while one was open for 25% -> 0% of each run, Pallas kernels for 0% -> 0%
where the time goes in v1:
time: 86.1 us; the launch traced here: 85.9 us
  Pallas kernels  76.8 us (89%)
  local copies, waits for them, and re-layouts  7.75 us (9%)
  between operations  1.32 us (2%)
    pallas_call x1, Pallas kernels, body(): pl.pallas_call(kernel, out_shape=(wide, wide, wide, narrow, narrow), in_s...  76.8 us
    unnamed x19, local copies, waits for them, and re-layouts  7.75 us

profile of v1, /device:TPU:1, one launch (start us, length us, event | category | flops | bytes accessed | tf_op | source)
XLA Modules:
  0.0 85.9 jit_solution(12460902969200341325)
XLA Ops:
  1.3 0.0 copy-start.4
  1.3 0.0 copy-start.5
  1.3 0.0 copy-start.6
  1.3 0.6 copy-done.4
  1.9 0.0 copy-done.5
  2.0 0.0 copy-done.6
  2.0 0.0 copy-start
  2.0 1.0 %copy-done = bf16[256,640]{1,0:T(8,128)(2,1)S(1)} copy-done((bf16[256,640]{1,0:T(8,128)(2,1)S(1)}, bf16[256,640]{1,0:T(8,128)(2,1)}, u32[]{:S(2)}) %copy-start) | copy-done | bytes 327704
  2.9 0.0 copy-start.1
  2.9 1.0 %copy-done.1 = bf16[256,640]{1,0:T(8,128)(2,1)S(1)} copy-done((bf16[256,640]{1,0:T(8,128)(2,1)S(1)}, bf16[256,640]{1,0:T(8,128)(2,1)}, u32[]{:S(2)}) %copy-start.1) | copy-done | bytes 327704
  3.9 0.0 copy-start.2
  3.9 1.0 %copy-done.2 = bf16[256,640]{1,0:T(8,128)(2,1)S(1)} copy-done((bf16[256,640]{1,0:T(8,128)(2,1)S(1)}, bf16[256,640]{1,0:T(8,128)(2,1)}, u32[]{:S(2)}) %copy-start.2) | copy-done | bytes 327704
  4.9 0.0 copy-start.3
  4.9 1.0 %copy-done.3 = bf16[256,640]{1,0:T(8,128)(2,1)S(1)} copy-done((bf16[256,640]{1,0:T(8,128)(2,1)S(1)}, bf16[256,640]{1,0:T(8,128)(2,1)}, u32[]{:S(2)}) %copy-start.3) | copy-done | bytes 327704
  5.9 76.8 %shard_map.119 = (bf16[256,640]{1,0:T(8,128)(2,1)S(1)}, bf16[256,640]{1,0:T(8,128)(2,1)S(1)}, bf16[256,640]{1,0:T(8,128)(2,1)S(1)}, f32[1,128]{1,0:T(1,128)S(1)}, f32[1,128]{1,0:T(1,128)S(1)}) custom-call(bf16[256,640]{1,0:T(8,128)(2,1)S(1)} %copy-done, bf16[256,640]{1,0:T(8,128)(2,1)S(1)} %copy-done.1, bf16[256,640]{1,0:T(8,128)(2,1)S(1)} %copy-done.2, ...), custom_call_target="tpu_custom_call" | custom-call | flops 1258291200 | bytes 2293760 | tf_op jit(solution)/shard_map/pallas_call | solution.py:295
  82.7 0.7 copy.19
  83.4 0.7 copy.20
  84.1 0.7 copy.21
  84.8 0.5 copy.22
  85.4 0.5 copy.23
Async XLA Ops:
  1.3 0.7 copy-start.4
  1.3 0.7 copy-start.5
  1.3 0.7 copy-start.6
  2.0 1.0 %copy-start = (bf16[256,640]{1,0:T(8,128)(2,1)S(1)}, bf16[256,640]{1,0:T(8,128)(2,1)}, u32[]{:S(2)}) copy-start(bf16[256,640]{1,0:T(8,128)(2,1)} %q_hbm.1) | copy-start | bytes 983044
  2.9 1.0 %copy-start.1 = (bf16[256,640]{1,0:T(8,128)(2,1)S(1)}, bf16[256,640]{1,0:T(8,128)(2,1)}, u32[]{:S(2)}) copy-start(bf16[256,640]{1,0:T(8,128)(2,1)} %k_hbm.1) | copy-start | bytes 983044
  3.9 1.0 %copy-start.2 = (bf16[256,640]{1,0:T(8,128)(2,1)S(1)}, bf16[256,640]{1,0:T(8,128)(2,1)}, u32[]{:S(2)}) copy-start(bf16[256,640]{1,0:T(8,128)(2,1)} %v_hbm.1) | copy-start | bytes 983044
  4.9 1.0 %copy-start.3 = (bf16[256,640]{1,0:T(8,128)(2,1)S(1)}, bf16[256,640]{1,0:T(8,128)(2,1)}, u32[]{:S(2)}) copy-start(bf16[256,640]{1,0:T(8,128)(2,1)} %g_hbm.1) | copy-start | bytes 983044

commit v2 on v1

--- a/solution.py
+++ b/solution.py
@@ -19,6 +19,9 @@
 Z_DEVS = 8
 PEERS = (HEAD_DEVS - 1) + (Y_DEVS - 1) + (Z_DEVS - 1)
 MESH = pl.DeviceIdType.MESH
+ORDER = (
+    "N0 Q0 N1 Q1 " "N2 N3 N4 K0 " "K1 K2 K3 K4 " "L0 L1 L2 L3 " "L4 F0 Q2 F1 " "C0 Q3 G0 F2 " "C1 Q4 G1 F3 " "C2 G2 B0 D0 " "H0 F4 C3 G3 " "B1 D1 H1 C4 " "G4 B2 D2 B3 " "B4 A0 D3 H2 " "H3 H4 E0 A1 " "D4 E1 W0 W1 " "A2 E2 W2 E3 " "W3 E4 W4 A3 "
+)
 NT = (((1,), (1,)), ((), ()))
 NN = (((1,), (0,)), ((), ()))
 TN = (((0,), (0,)), ((), ()))
@@ -30,10 +33,10 @@
 
 def kernel(
     q_hbm, k_hbm, v_hbm, g_hbm, gain_q_ref, gain_k_ref, blocks_ref, count_ref,
-    oq_hbm, ok_hbm, ov_hbm, ogain_q_ref, ogain_k_ref,
+    oq_hbm, ok_hbm, ov_hbm, ogain_ref,
     raw_q, raw_k, qn, kn, vn, gn, rq, rg,
     q_hat, q_inv, k_hat, k_inv, prob, dprob, stat_own, stat_out, stat_in,
-    fin_own, fin_out, fin_in, dq_own, dq_out, dq_in, oq, ok, ov, acc,
+    fin_own, fin_out, fin_in, dq_own, dk_sum, dv_sum, dq_out, dq_in, oq, ok, ov, acc,
     sum_a, sum_b, sum_c,
     load_sem, store_sem, qs, qr, gs, gr, ss, sr, fs, fr, ds, dr, as_, ar,
 ):
@@ -103,19 +106,23 @@
         inv[h] = jnp.broadcast_to(inverse, x.shape)
         normed[h] = (x_hat * gain).astype(jnp.bfloat16)
 
-    for h in range(HEADS):
+    def norm_query(h):
         load(q_hbm, raw_q, 1, h).wait()
         load(g_hbm, gn, 0, h).wait()
         norm(raw_q, gain_q, q_hat, q_inv, qn, h)
+
+    def send(h):
         if h == 0:
             pl.semaphore_wait(barrier, PEERS)
         for i in (1, 0):
             g_copy(h, i).start()
             q_copy(h, i).start()
-    for h in range(HEADS):
+
+    def norm_key(h):
         load(k_hbm, raw_k, 2, h).wait()
         load(v_hbm, vn, 3, h).wait()
         norm(raw_k, gain_k, k_hat, k_inv, kn, h)
+
     acc[...] = jnp.zeros_like(acc)
 
     def forward(h, slot, query, grad):
@@ -180,48 +187,41 @@
         return jnp.sum(a.reshape(ROWS // 8, 8, HEAD_DIM), axis=0)
 
     def columns(h):
-        return pl.ds(pl.multiple_of(h * HEAD_DIM, HEAD_DIM), HEAD_DIM)
+        return slice(h * HEAD_DIM, (h + 1) * HEAD_DIM)
 
     def store(src, dst, slot, h):
         return pltpu.make_async_copy(src.at[h], dst.at[:, columns(h)], store_sem.at[slot, h])
 
-    def backward(h):
-        for i in range(BITS):
+    def near_back(h):
+        dq, dk, dv = one_back(h, 0, qn[h], gn[h], fin_own[h, 0:1], fin_own[h, 1:2])
+        dq_own[h] = dq
+        dk_sum[h] = dk
+        dv_sum[h] = dv
+        acc[0] += fold(dq * q_hat[h])
+
+    def far_back(h):
+        gk, gv = dk_sum[h], dv_sum[h]
+        for i in (1, 0):
             f_copy(h, i).wait_recv()
             dq, dk, dv = one_back(
                 h, i + 1, rq[i, h], rg[i, h], fin_in[i, h, 0:1], fin_in[i, h, 1:2]
             )
             dq_out[i, h] = dq.astype(jnp.bfloat16)
+            acc[1] += fold(dq * rq[i, h].astype(jnp.float32))
+            gk, gv = gk + dk, gv + dv
+        dk_sum[h] = gk
+        dv_sum[h] = gv
+        acc[2] += fold(gk * k_hat[h])
+
+    def write_kv(h):
+        ov[h] = dv_sum[h].astype(jnp.bfloat16)
+        store(ov, ov_hbm, 2, h).start()
+        ok[h] = norm_back(k_hat[h], k_inv[h], gain_k, dk_sum[h])
+        store(ok, ok_hbm, 1, h).start()
+
+    def send_dq(h):
+        for i in (1, 0):
             d_copy(h, i).start()
-            acc[1] += fold(dq * rq[i, h].astype(jnp.float32))
-            if i == 0:
-                gk, gv = dk, dv
-            else:
-                gk, gv = gk + dk, gv + dv
-        dq, dk, dv = one_back(h, 0, qn[h], gn[h], fin_own[h, 0:1], fin_own[h, 1:2])
-        gk, gv = gk + dk, gv + dv
-        dq_own[h] = dq
-        acc[0] += fold(dq * q_hat[h])
-        acc[2] += fold(gk * k_hat[h])
-        ov[h] = gv.astype(jnp.bfloat16)
-        store(ov, ov_hbm, 2, h).start()
-        ok[h] = norm_back(k_hat[h], k_inv[h], gain_k, gk)
-        store(ok, ok_hbm, 1, h).start()
-
-    def step(h, carry):
-        @pl.when(h < HEADS)
-        def _():
-            far_forward(h)
-            near_forward(h)
-            combine(h)
-
-        @pl.when(h > 0)
-        def _():
-            backward(h - 1)
-
-        return carry
-
-    lax.fori_loop(0, HEADS + 1, step, 0)
 
     def finish(h):
         for i in range(BITS):
@@ -240,43 +240,61 @@
     copies_b = share_copies(sum_b, y, y_peers, HEAD_DEVS - 1)
     copies_c = share_copies(sum_c, z, z_peers, HEAD_DEVS + Y_DEVS - 2)
 
-    part_q = jnp.sum(acc[0], axis=0, keepdims=True) + jnp.sum(acc[1], axis=0, keepdims=True) / gain_q
-    sum_a[column, 0:1] = part_q
-    sum_a[column, 1:2] = jnp.sum(acc[2], axis=0, keepdims=True)
-    for c in copies_a:
-        c.start()
-    finish(0)
-    finish(1)
-    for c in copies_a:
-        c.wait_recv()
-    sum_b[y] = jnp.sum(sum_a[...], axis=0)
-    for c in copies_b:
-        c.start()
-    finish(2)
-    for c in copies_b:
-        c.wait_recv()
-    sum_c[z] = jnp.sum(sum_b[...], axis=0)
-    for c in copies_c:
-        c.start()
-    finish(3)
-    finish(4)
-    for c in copies_c:
-        c.wait_recv()
-    total = jnp.sum(sum_c[...], axis=0)
-    ogain_q_ref[...] = total[0:1]
-    ogain_k_ref[...] = total[1:2]
-
-    for c in copies_a + copies_b + copies_c:
-        c.wait_send()
-    for h in range(HEADS):
+    def gain_sums(stage):
+        if stage == 0:
+            part_q = jnp.sum(acc[0], axis=0, keepdims=True)
+            part_q += jnp.sum(acc[1], axis=0, keepdims=True) / gain_q
+            sum_a[column, 0:1] = part_q
+            sum_a[column, 1:2] = jnp.sum(acc[2], axis=0, keepdims=True)
+            for c in copies_a:
+                c.start()
+        elif stage == 1:
+            for c in copies_a:
+                c.wait_recv()
+            sum_b[y] = jnp.sum(sum_a[...], axis=0)
+            for c in copies_b:
+                c.start()
+        elif stage == 2:
+            for c in copies_a:
+                c.wait_send()
+            for c in copies_b:
+                c.wait_recv()
+            sum_c[z] = jnp.sum(sum_b[...], axis=0)
+            for c in copies_c:
+                c.start()
+        else:
+            for c in copies_b:
+                c.wait_send()
+            for c in copies_c:
+                c.wait_recv()
+            total = jnp.sum(sum_c[...], axis=0)
+            ogain_ref[...] = total
+
+    def wait_sent(h):
         for i in range(BITS):
-            q_copy(h, i).wait_send()
-            g_copy(h, i).wait_send()
-            s_copy(h, i).wait_send()
-            f_copy(h, i).wait_send()
-            d_copy(h, i).wait_send()
+            for copy in (q_copy, g_copy, s_copy, f_copy, d_copy):
+                copy(h, i).wait_send()
         for slot, (src, dst) in enumerate(((oq, oq_hbm), (ok, ok_hbm), (ov, ov_hbm))):
             store(src, dst, slot, h).wait()
+
+    steps = {
+        "N": norm_query, "Q": send, "K": norm_key, "L": near_forward, "F": far_forward,
+        "C": combine, "G": near_back, "B": far_back, "H": write_kv, "W": wait_sent, "D": send_dq, "E": finish, "A": gain_sums,
+    }
+    for word in ORDER.split():
+        steps[word[0]](int(word[1]))
+
+    for c in copies_c:
+        c.wait_send()
+
+
+def hand_over(q, k, v, gains, oq, ok, ov, ogain_q, ogain_k, sem):
+    pairs = ((q, oq), (k, ok), (v, ov), (gains.at[0:1], ogain_q), (gains.at[1:2], ogain_k))
+    copies = [pltpu.make_async_copy(src, dst, sem.at[n]) for n, (src, dst) in enumerate(pairs)]
+    for c in copies:
+        c.start()
+    for c in copies:
+        c.wait()
 
 
 def body(q_raw, k_raw, values, grad_out, gain_q, gain_k, pair_blocks, pair_count):
@@ -292,11 +310,11 @@
     in_vmem = pl.BlockSpec(memory_space=pltpu.VMEM)
     in_smem = pl.BlockSpec(memory_space=pltpu.SMEM)
     pair = pltpu.SemaphoreType.DMA((BITS, HEADS))
-    grad_q, grad_k, grad_v, sum_q, sum_k = pl.pallas_call(
+    parts = pl.pallas_call(
         kernel,
-        out_shape=(wide, wide, wide, narrow, narrow),
+        out_shape=(wide, wide, wide, jax.ShapeDtypeStruct((2, HEAD_DIM), jnp.float32)),
         in_specs=[any_space] * 4 + [in_vmem] * 2 + [in_smem] * 2,
-        out_specs=(any_space, any_space, any_space, in_vmem, in_vmem),
+        out_specs=(any_space, any_space, any_space, in_vmem),
         scratch_shapes=[
             vmem(*tile, dtype=low), vmem(*tile, dtype=low),
             vmem(*tile, dtype=low), vmem(*tile, dtype=low), vmem(*tile, dtype=low), vmem(*tile, dtype=low),
@@ -305,7 +323,7 @@
             vmem(*square), vmem(*square),
             vmem(HEADS, 2, ROWS), vmem(BITS, HEADS, 2, ROWS), vmem(BITS, HEADS, 2, ROWS),
             vmem(HEADS, 2, ROWS), vmem(BITS, HEADS, 2, ROWS), vmem(BITS, HEADS, 2, ROWS),
-            vmem(*tile), vmem(BITS, *tile, dtype=low), vmem(BITS, *tile, dtype=low),
+            vmem(*tile), vmem(*tile), vmem(*tile), vmem(BITS, *tile, dtype=low), vmem(BITS, *tile, dtype=low),
             vmem(*tile, dtype=low), vmem(*tile, dtype=low), vmem(*tile, dtype=low),
             vmem(3, 8, HEAD_DIM),
             vmem(HEAD_DEVS, 2, HEAD_DIM), vmem(Y_DEVS, 2, HEAD_DIM), vmem(Z_DEVS, 2, HEAD_DIM),
@@ -314,7 +332,7 @@
             pltpu.SemaphoreType.DMA((PEERS,)), pltpu.SemaphoreType.DMA((PEERS,)),
         ],
         compiler_params=pltpu.CompilerParams(
-            collective_id=0, has_side_effects=True, vmem_limit_bytes=40 * 1024 * 1024
+            collective_id=0, has_side_effects=True, vmem_limit_bytes=63 * 1024 * 1024
         ),
         cost_estimate=pl.CostEstimate(
             flops=2 * 5 * 15 * ROWS * ROWS * HEAD_DIM,
@@ -325,6 +343,14 @@
         q_raw, k_raw, values, grad_out,
         gain_q.reshape(1, HEAD_DIM), gain_k.reshape(1, HEAD_DIM), pair_blocks, pair_count,
     )
+    grad_q, grad_k, grad_v, sum_q, sum_k = pl.pallas_call(
+        hand_over,
+        out_shape=(wide, wide, wide, narrow, narrow),
+        in_specs=[in_vmem] * 4,
+        out_specs=(any_space,) * 5,
+        scratch_shapes=[pltpu.SemaphoreType.DMA((5,))],
+        compiler_params=pltpu.CompilerParams(has_side_effects=True, vmem_limit_bytes=63 * 1024 * 1024),
+    )(*parts)
     return grad_q, grad_k, grad_v, sum_q.reshape(HEAD_DIM), sum_k.reshape(HEAD_DIM)
 
 

time: 86.1 us -> 65.3 us (0.76)
  Pallas kernels: 76.8 us -> 63.8 us
  local copies, waits for them, and re-layouts: 7.75 us -> 0 us
    pallas_call x1 -> x2, Pallas kernels: 76.8 us -> 63.8 us  [the longest x1 61.6 us: body(): pl.pallas_call(kernel, out_shape=(wide, wide, wide, jax.ShapeDtypeStruct(...]
    unnamed x19 -> x0, local copies, waits for them, and re-layouts: 7.75 us -> none
where the time goes in v2:
time: 65.3 us; the launch traced here: 65.1 us
  Pallas kernels  63.8 us (98%)
  between operations  1.29 us (2%)
    pallas_call x1, Pallas kernels, body(): pl.pallas_call(kernel, out_shape=(wide, wide, wide, jax.ShapeDtypeStruct(...  61.6 us
    pallas_call x1, Pallas kernels, body(): pl.pallas_call(hand_over, out_shape=(wide, wide, wide, narrow, narrow), i...  2.16 us

profile of v2, /device:TPU:1, one launch (start us, length us, event | category | flops | bytes accessed | tf_op | source)
XLA Modules:
  0.0 65.1 jit_solution(4035955289097355776)
XLA Ops:
  1.3 61.6 %shard_map.119 = (bf16[256,640]{1,0:T(8,128)(2,1)}, bf16[256,640]{1,0:T(8,128)(2,1)}, bf16[256,640]{1,0:T(8,128)(2,1)}, f32[2,128]{1,0:T(2,128)}) custom-call(bf16[256,640]{1,0:T(8,128)(2,1)} %q_hbm.1, bf16[256,640]{1,0:T(8,128)(2,1)} %k_hbm.1, bf16[256,640]{1,0:T(8,128)(2,1)} %v_hbm.1, bf16[256,640]{1,0:T(8,128)(2,1)} %g_hbm.1, f32[1,128]{1,0:T(1,128)} %bitcast.4, ...), custom_call_target="tpu_custom_call" | custom-call | flops 1258291200 | bytes 2293760 | tf_op jit(solution)/shard_map/pallas_call | solution.py:313
  62.9 2.2 %shard_map.120 = (bf16[256,640]{1,0:T(8,128)(2,1)}, bf16[256,640]{1,0:T(8,128)(2,1)}, bf16[256,640]{1,0:T(8,128)(2,1)}, f32[1,128]{1,0:T(1,128)}, f32[1,128]{1,0:T(1,128)}) custom-call(bf16[256,640]{1,0:T(8,128)(2,1)} %get-tuple-element.14.q, bf16[256,640]{1,0:T(8,128)(2,1)} %get-tuple-element.15.k, bf16[256,640]{1,0:T(8,128)(2,1)} %get-tuple-element.16.v, ...), custom_call_target="tpu_custom_call" | custom-call | tf_op jit(solution)/shard_map/pallas_call | solution.py:346

commit v3 on v2

--- a/solution.py
+++ b/solution.py
@@ -17,10 +17,26 @@
 HEAD_DEVS = 8
 Y_DEVS = 4
 Z_DEVS = 8
+PIECES = 1
 PEERS = (HEAD_DEVS - 1) + (Y_DEVS - 1) + (Z_DEVS - 1)
 MESH = pl.DeviceIdType.MESH
 ORDER = (
-    "N0 Q0 N1 Q1 " "N2 N3 N4 K0 " "K1 K2 K3 K4 " "L0 L1 L2 L3 " "L4 F0 Q2 F1 " "C0 Q3 G0 F2 " "C1 Q4 G1 F3 " "C2 G2 B0 D0 " "H0 F4 C3 G3 " "B1 D1 H1 C4 " "G4 B2 D2 B3 " "B4 A0 D3 H2 " "H3 H4 E0 A1 " "D4 E1 W0 W1 " "A2 E2 W2 E3 " "W3 E4 W4 A3 "
+    "N0 Q0 N1 Q1",
+    "N2 N3 N4 K0",
+    "K1 K2 K3 K4",
+    "L0 L1 L2 L3",
+    "L4 F0 Q2 F1",
+    "C0 Q3 G0 F2",
+    "C1 Q4 G1 F3",
+    "C2 G2 B0 D0",
+    "H0 F4 C3 G3",
+    "B1 D1 H1 C4",
+    "G4 B2 D2 B3",
+    "B4 A0 D3 H2",
+    "H3 H4 E0 A1",
+    "D4 E1 W0 W1",
+    "A2 E2 W2 E3",
+    "W3 E4 W4 A3",
 )
 NT = (((1,), (1,)), ((), ()))
 NN = (((1,), (0,)), ((), ()))
@@ -281,8 +297,9 @@
         "N": norm_query, "Q": send, "K": norm_key, "L": near_forward, "F": far_forward,
         "C": combine, "G": near_back, "B": far_back, "H": write_kv, "W": wait_sent, "D": send_dq, "E": finish, "A": gain_sums,
     }
-    for word in ORDER.split():
-        steps[word[0]](int(word[1]))
+    for line in ORDER:
+        for word in line.split():
+            steps[word[0]](int(word[1]))
 
     for c in copies_c:
         c.wait_send()
@@ -312,7 +329,7 @@
     pair = pltpu.SemaphoreType.DMA((BITS, HEADS))
     parts = pl.pallas_call(
         kernel,
-        out_shape=(wide, wide, wide, jax.ShapeDtypeStruct((2, HEAD_DIM), jnp.float32)),
+        out_shape=(pltpu.VMEM((ROWS, HEADS * HEAD_DIM), low),) * 3 + (pltpu.VMEM((2, HEAD_DIM), jnp.float32),),
         in_specs=[any_space] * 4 + [in_vmem] * 2 + [in_smem] * 2,
         out_specs=(any_space, any_space, any_space, in_vmem),
         scratch_shapes=[
@@ -332,7 +349,7 @@
             pltpu.SemaphoreType.DMA((PEERS,)), pltpu.SemaphoreType.DMA((PEERS,)),
         ],
         compiler_params=pltpu.CompilerParams(
-            collective_id=0, has_side_effects=True, vmem_limit_bytes=63 * 1024 * 1024
+            collective_id=0, has_side_effects=True, vmem_limit_bytes=56 * 1024 * 1024
         ),
         cost_estimate=pl.CostEstimate(
             flops=2 * 5 * 15 * ROWS * ROWS * HEAD_DIM,
@@ -340,16 +357,19 @@
             transcendentals=15 * ROWS * ROWS,
         ),
     )(
-        q_raw, k_raw, values, grad_out,
-        gain_q.reshape(1, HEAD_DIM), gain_k.reshape(1, HEAD_DIM), pair_blocks, pair_count,
+        *[
+            pltpu.with_memory_space_constraint(x, pltpu.HBM)
+            for x in (q_raw, k_raw, values, grad_out, gain_q.reshape(1, HEAD_DIM), gain_k.reshape(1, HEAD_DIM))
+        ],
+        pair_blocks, pair_count,
     )
     grad_q, grad_k, grad_v, sum_q, sum_k = pl.pallas_call(
         hand_over,
         out_shape=(wide, wide, wide, narrow, narrow),
-        in_specs=[in_vmem] * 4,
+        in_specs=[any_space] * 4,
         out_specs=(any_space,) * 5,
         scratch_shapes=[pltpu.SemaphoreType.DMA((5,))],
-        compiler_params=pltpu.CompilerParams(has_side_effects=True, vmem_limit_bytes=63 * 1024 * 1024),
+        compiler_params=pltpu.CompilerParams(has_side_effects=True, vmem_limit_bytes=16 * 1024 * 1024),
     )(*parts)
     return grad_q, grad_k, grad_v, sum_q.reshape(HEAD_DIM), sum_k.reshape(HEAD_DIM)
 

time: 65.3 us -> 63.5 us (0.972)
  Pallas kernels: 63.8 us -> 62.1 us
    pallas_call x1, Pallas kernels: 2.16 us -> 0.99 us  [body(): pl.pallas_call(hand_over, out_shape=(wide, wide, wide, narrow, narrow), i...]
where the time goes in v3:
time: 63.5 us; the launch traced here: 63.4 us
  Pallas kernels  62.1 us (98%)
  between operations  1.29 us (2%)
    pallas_call x1, Pallas kernels, body(): pl.pallas_call(kernel, out_shape=(pltpu.VMEM((ROWS, HEADS * HEAD_DIM), lo...  61.1 us

profile of v3, /device:TPU:1, one launch (start us, length us, event | category | flops | bytes accessed | tf_op | source)
XLA Modules:
  0.0 63.4 jit_solution(3277964594229943025)
XLA Ops:
  1.3 61.1 %shard_map.119 = (bf16[256,640]{1,0:T(8,128)(2,1)S(1)}, bf16[256,640]{1,0:T(8,128)(2,1)S(1)}, bf16[256,640]{1,0:T(8,128)(2,1)S(1)}, f32[2,128]{1,0:T(2,128)S(1)}) custom-call(bf16[256,640]{1,0:T(8,128)(2,1)} %q_hbm.1, bf16[256,640]{1,0:T(8,128)(2,1)} %k_hbm.1, bf16[256,640]{1,0:T(8,128)(2,1)} %v_hbm.1, bf16[256,640]{1,0:T(8,128)(2,1)} %g_hbm.1, ...), custom_call_target="tpu_custom_call" | custom-call | flops 1258291200 | bytes 2293760 | tf_op jit(solution)/shard_map/pallas_call | solution.py:330
  62.4 1.0 %shard_map.120 = (bf16[256,640]{1,0:T(8,128)(2,1)}, bf16[256,640]{1,0:T(8,128)(2,1)}, bf16[256,640]{1,0:T(8,128)(2,1)}, f32[1,128]{1,0:T(1,128)}, f32[1,128]{1,0:T(1,128)}) custom-call(bf16[256,640]{1,0:T(8,128)(2,1)S(1)} %get-tuple-element.14.q, bf16[256,640]{1,0:T(8,128)(2,1)S(1)} %get-tuple-element.15.k, bf16[256,640]{1,0:T(8,128)(2,1)S(1)} %get-tuple-element.16.v, ...), custom_call_target="tpu_custom_call" | custom-call | tf_op jit(solution)/shard_map/pallas_call | solution.py:366

commit v4 on v3

--- a/solution.py
+++ b/solution.py
@@ -17,26 +17,27 @@
 HEAD_DEVS = 8
 Y_DEVS = 4
 Z_DEVS = 8
-PIECES = 1
 PEERS = (HEAD_DEVS - 1) + (Y_DEVS - 1) + (Z_DEVS - 1)
 MESH = pl.DeviceIdType.MESH
 ORDER = (
-    "N0 Q0 N1 Q1",
-    "N2 N3 N4 K0",
-    "K1 K2 K3 K4",
-    "L0 L1 L2 L3",
-    "L4 F0 Q2 F1",
-    "C0 Q3 G0 F2",
-    "C1 Q4 G1 F3",
-    "C2 G2 B0 D0",
-    "H0 F4 C3 G3",
-    "B1 D1 H1 C4",
-    "G4 B2 D2 B3",
-    "B4 A0 D3 H2",
-    "H3 H4 E0 A1",
-    "D4 E1 W0 W1",
-    "A2 E2 W2 E3",
-    "W3 E4 W4 A3",
+    "N0 Q0 J0 J1",
+    "J2 J3 J4 N1",
+    "Q1 N2 N3 N4",
+    "K0 K1 K2 K3",
+    "K4 L0 L1 L2",
+    "L3 L4 M0 F0",
+    "Q2 F1 C0 Q3",
+    "G0 F2 V0 B0",
+    "C1 Q4 G1 B1",
+    "F3 C2 G2 B2",
+    "F4 D0 D1 H0",
+    "C3 G3 B3 C4",
+    "G4 B4 A0 D2",
+    "H1 H2 H3 H4",
+    "E0 A1 D3 E1",
+    "W0 W1 A2 D4",
+    "E2 W2 E3 W3",
+    "E4 W4 A3",
 )
 NT = (((1,), (1,)), ((), ()))
 NN = (((1,), (0,)), ((), ()))
@@ -51,21 +52,22 @@
     q_hbm, k_hbm, v_hbm, g_hbm, gain_q_ref, gain_k_ref, blocks_ref, count_ref,
     oq_hbm, ok_hbm, ov_hbm, ogain_ref,
     raw_q, raw_k, qn, kn, vn, gn, rq, rg,
-    q_hat, q_inv, k_hat, k_inv, prob, dprob, stat_own, stat_out, stat_in,
-    fin_own, fin_out, fin_in, dq_own, dk_sum, dv_sum, dq_out, dq_in, oq, ok, ov, acc,
+    q_hat, q_inv, k_hat, k_inv, prob, dprob, near_out, near_in,
+    stat_out, stat_in, cross_in, fin_own, dq_own, dk_sum, dv_sum, dq_out, dq_in, oq, ok, ov, acc,
     sum_a, sum_b, sum_c,
-    load_sem, store_sem, qs, qr, gs, gr, ss, sr, fs, fr, ds, dr, as_, ar,
+    load_sem, store_sem, qs, qr, gs, gr, ss, sr, ns, nr, xs, xr, ds, dr, as_, ar,
 ):
     place = lax.axis_index("ctx")
     column = lax.axis_index("head")
     z = lax.rem(place, Z_DEVS)
     y = lax.div(place, Z_DEVS)
     partners = [jnp.bitwise_xor(place, 1 << i) for i in range(BITS)]
+    across = {"ctx": jnp.bitwise_xor(place, 3)}
     lower = [jnp.bitwise_and(place, 1 << i) == 0 for i in range(BITS)]
 
-    head_peers = [{"head": lax.rem(column + r, HEAD_DEVS)} for r in range(1, HEAD_DEVS)]
-    y_peers = [{"ctx": lax.rem(y + r, Y_DEVS) * Z_DEVS + z} for r in range(1, Y_DEVS)]
-    z_peers = [{"ctx": y * Z_DEVS + lax.rem(z + r, Z_DEVS)} for r in range(1, Z_DEVS)]
+    head_peers = [{"head": lax.rem(column + r, HEAD_DEVS)} for r in (4, 5, 3, 2, 6, 1, 7)]
+    y_peers = [{"ctx": lax.rem(y + r, Y_DEVS) * Z_DEVS + z} for r in (2, 1, 3)]
+    z_peers = [{"ctx": y * Z_DEVS + lax.rem(z + r, Z_DEVS)} for r in (4, 3, 5, 2, 6, 1, 7)]
 
     barrier = pltpu.get_barrier_semaphore()
     for peer in z_peers + y_peers + head_peers:
@@ -76,10 +78,9 @@
             src.at[:, h * HEAD_DIM : (h + 1) * HEAD_DIM], dst.at[h], load_sem.at[slot, h]
         )
 
-    sources = ((g_hbm, gn), (q_hbm, raw_q), (k_hbm, raw_k), (v_hbm, vn))
-    for slot, (src, dst) in enumerate(sources):
-        for h in range(HEADS):
-            load(src, dst, slot, h).start()
+    for h in range(HEADS):
+        load(g_hbm, gn, 0, h).start()
+        load(q_hbm, raw_q, 1, h).start()
 
     def remote(src, dst, send, recv, peer):
         return pltpu.make_async_remote_copy(
@@ -94,10 +95,13 @@
         return remote(gn.at[h], rg.at[i, h], gs.at[i, h], gr.at[i, h], {"ctx": partners[i]})
 
     def s_copy(h, i):
-        return remote(stat_out.at[i, h], stat_in.at[i, h], ss.at[i, h], sr.at[i, h], {"ctx": partners[i]})
-
-    def f_copy(h, i):
-        return remote(fin_out.at[i, h], fin_in.at[i, h], fs.at[i, h], fr.at[i, h], {"ctx": partners[i]})
+        return remote(stat_out.at[h, i], stat_in.at[h, i], ss.at[i, h], sr.at[i, h], {"ctx": partners[i]})
+
+    def x_copy(h):
+        return remote(stat_out.at[h], cross_in.at[h], xs.at[h], xr.at[h], across)
+
+    def n_copy(i):
+        return remote(near_out, near_in.at[i], ns.at[i], nr.at[i], {"ctx": partners[i]})
 
     def d_copy(h, i):
         return remote(dq_out.at[i, h], dq_in.at[i, h], ds.at[i, h], dr.at[i, h], {"ctx": partners[i]})
@@ -133,6 +137,10 @@
         for i in (1, 0):
             g_copy(h, i).start()
             q_copy(h, i).start()
+
+    def load_kv(h):
+        load(k_hbm, raw_k, 2, h).start()
+        load(v_hbm, vn, 3, h).start()
 
     def norm_key(h):
         load(k_hbm, raw_k, 2, h).wait()
@@ -158,33 +166,52 @@
             g_copy(h, i).wait_recv()
             q_copy(h, i).wait_recv()
             log, dot = forward(h, i + 1, rq[i, h], rg[i, h])
-            stat_out[i, h, 0:1] = jnp.where(off[i] > 0.5, FLOOR_LOG, log)
-            stat_out[i, h, 1:2] = dot
+            stat_out[h, i, 0:1] = jnp.where(off[i] > 0.5, FLOOR_LOG, log)
+            stat_out[h, i, 1:2] = dot
+            if i == 1:
+                x_copy(h).start()
             s_copy(h, i).start()
 
     def near_forward(h):
         log, dot = forward(h, 0, qn[h], gn[h])
-        stat_own[h, 0:1] = log
-        stat_own[h, 1:2] = dot
-
-    def combine(h):
-        logs = [stat_own[h, 0:1]]
-        dots = [stat_own[h, 1:2]]
+        near_out[h, 0:1] = log
+        near_out[h, 1:2] = dot
         for i in range(BITS):
-            s_copy(h, i).wait_recv()
-            logs.append(jnp.where(off[i] > 0.5, FLOOR_LOG, stat_in[i, h, 0:1]))
-            dots.append(stat_in[i, h, 1:2])
+            near_out[h, 2 + i : 3 + i] = jnp.full((1, ROWS), off[i], jnp.float32)
+
+    def send_near(h):
+        for i in (1, 0):
+            n_copy(i).start()
+
+    def wait_near(h):
+        for i in range(BITS):
+            n_copy(i).wait_recv()
+
+    def shares_of(logs, dots):
         top = jnp.maximum(jnp.maximum(logs[0], logs[1]), logs[2])
         parts = [jnp.exp(log - top) for log in logs]
         inverse = 1.0 / (parts[0] + parts[1] + parts[2])
-        shares = [part * inverse for part in parts]
-        row_dot = shares[0] * dots[0] + shares[1] * dots[1] + shares[2] * dots[2]
+        row_dot = (parts[0] * dots[0] + parts[1] * dots[1] + parts[2] * dots[2]) * inverse
+        return parts[0] * inverse, row_dot
+
+    def combine(h):
+        logs = [near_out[h, 0:1]]
+        dots = [near_out[h, 1:2]]
         for i in range(BITS):
-            fin_out[i, h, 0:1] = shares[i + 1]
-            fin_out[i, h, 1:2] = row_dot
-            f_copy(h, i).start()
-        fin_own[h, 0:1] = shares[0]
-        fin_own[h, 1:2] = row_dot
+            s_copy(h, i).wait_recv()
+            logs.append(jnp.where(off[i] > 0.5, FLOOR_LOG, stat_in[h, i, 0:1]))
+            dots.append(stat_in[h, i, 1:2])
+        fin_own[h, 0:1], fin_own[h, 1:2] = shares_of(logs, dots)
+
+    def far_shares(h, i):
+        other = 1 - i
+        logs = [
+            jnp.where(near_in[i, h, 2 + i : 3 + i] > 0.5, FLOOR_LOG, stat_out[h, i, 0:1]),
+            near_in[i, h, 0:1],
+            jnp.where(near_in[i, h, 2 + other : 3 + other] > 0.5, FLOOR_LOG, cross_in[h, other, 0:1]),
+        ]
+        dots = [stat_out[h, i, 1:2], near_in[i, h, 1:2], cross_in[h, other, 1:2]]
+        return shares_of(logs, dots)
 
     def one_back(h, slot, query, grad, share, row_dot):
         w = prob[slot, h] * share
@@ -217,11 +244,10 @@
 
     def far_back(h):
         gk, gv = dk_sum[h], dv_sum[h]
+        x_copy(h).wait_recv()
         for i in (1, 0):
-            f_copy(h, i).wait_recv()
-            dq, dk, dv = one_back(
-                h, i + 1, rq[i, h], rg[i, h], fin_in[i, h, 0:1], fin_in[i, h, 1:2]
-            )
+            share, row_dot = far_shares(h, i)
+            dq, dk, dv = one_back(h, i + 1, rq[i, h], rg[i, h], share, row_dot)
             dq_out[i, h] = dq.astype(jnp.bfloat16)
             acc[1] += fold(dq * rq[i, h].astype(jnp.float32))
             gk, gv = gk + dk, gv + dv
@@ -288,14 +314,18 @@
 
     def wait_sent(h):
         for i in range(BITS):
-            for copy in (q_copy, g_copy, s_copy, f_copy, d_copy):
+            for copy in (q_copy, g_copy, s_copy, d_copy):
                 copy(h, i).wait_send()
+        x_copy(h).wait_send()
+        if h == 0:
+            for i in range(BITS):
+                n_copy(i).wait_send()
         for slot, (src, dst) in enumerate(((oq, oq_hbm), (ok, ok_hbm), (ov, ov_hbm))):
             store(src, dst, slot, h).wait()
 
     steps = {
         "N": norm_query, "Q": send, "K": norm_key, "L": near_forward, "F": far_forward,
-        "C": combine, "G": near_back, "B": far_back, "H": write_kv, "W": wait_sent, "D": send_dq, "E": finish, "A": gain_sums,
+        "C": combine, "J": load_kv, "M": send_near, "V": wait_near, "G": near_back, "B": far_back, "H": write_kv, "W": wait_sent, "D": send_dq, "E": finish, "A": gain_sums,
     }
     for line in ORDER:
         for word in line.split():
@@ -338,14 +368,17 @@
             vmem(BITS, *tile, dtype=low), vmem(BITS, *tile, dtype=low),
             vmem(*tile), vmem(*tile), vmem(*tile), vmem(*tile),
             vmem(*square), vmem(*square),
-            vmem(HEADS, 2, ROWS), vmem(BITS, HEADS, 2, ROWS), vmem(BITS, HEADS, 2, ROWS),
-            vmem(HEADS, 2, ROWS), vmem(BITS, HEADS, 2, ROWS), vmem(BITS, HEADS, 2, ROWS),
+            vmem(HEADS, 4, ROWS), vmem(BITS, HEADS, 4, ROWS),
+            vmem(HEADS, BITS, 2, ROWS), vmem(HEADS, BITS, 2, ROWS), vmem(HEADS, BITS, 2, ROWS),
+            vmem(HEADS, 2, ROWS),
             vmem(*tile), vmem(*tile), vmem(*tile), vmem(BITS, *tile, dtype=low), vmem(BITS, *tile, dtype=low),
             vmem(*tile, dtype=low), vmem(*tile, dtype=low), vmem(*tile, dtype=low),
             vmem(3, 8, HEAD_DIM),
             vmem(HEAD_DEVS, 2, HEAD_DIM), vmem(Y_DEVS, 2, HEAD_DIM), vmem(Z_DEVS, 2, HEAD_DIM),
             pltpu.SemaphoreType.DMA((4, HEADS)), pltpu.SemaphoreType.DMA((3, HEADS)),
-            pair, pair, pair, pair, pair, pair, pair, pair, pair, pair,
+            pair, pair, pair, pair, pair, pair,
+            pltpu.SemaphoreType.DMA((BITS,)), pltpu.SemaphoreType.DMA((BITS,)),
+            pltpu.SemaphoreType.DMA((HEADS,)), pltpu.SemaphoreType.DMA((HEADS,)), pair, pair,
             pltpu.SemaphoreType.DMA((PEERS,)), pltpu.SemaphoreType.DMA((PEERS,)),
         ],
         compiler_params=pltpu.CompilerParams(

time: 63.5 us -> 61.8 us (0.973)
  Pallas kernels: 62.1 us -> 60.3 us
    pallas_call x1, Pallas kernels: 61.1 us -> 59.3 us  [body(): pl.pallas_call(kernel, out_shape=(pltpu.VMEM((ROWS, HEADS * HEAD_DIM), lo...]
where the time goes in v4:
time: 61.8 us; the launch traced here: 61.6 us
  Pallas kernels  60.3 us (98%)
  between operations  1.29 us (2%)
    pallas_call x1, Pallas kernels, body(): pl.pallas_call(kernel, out_shape=(pltpu.VMEM((ROWS, HEADS * HEAD_DIM), lo...  59.3 us

profile of v4, /device:TPU:1, one launch (start us, length us, event | category | flops | bytes accessed | tf_op | source)
XLA Modules:
  0.0 61.6 jit_solution(1246815248539211829)
XLA Ops:
  1.3 59.3 %shard_map.119 = (bf16[256,640]{1,0:T(8,128)(2,1)S(1)}, bf16[256,640]{1,0:T(8,128)(2,1)S(1)}, bf16[256,640]{1,0:T(8,128)(2,1)S(1)}, f32[2,128]{1,0:T(2,128)S(1)}) custom-call(bf16[256,640]{1,0:T(8,128)(2,1)} %q_hbm.1, bf16[256,640]{1,0:T(8,128)(2,1)} %k_hbm.1, bf16[256,640]{1,0:T(8,128)(2,1)} %v_hbm.1, bf16[256,640]{1,0:T(8,128)(2,1)} %g_hbm.1, ...), custom_call_target="tpu_custom_call" | custom-call | flops 1258291200 | bytes 2293760 | tf_op jit(solution)/shard_map/pallas_call | solution.py:360
  60.6 1.0 %shard_map.120 = (bf16[256,640]{1,0:T(8,128)(2,1)}, bf16[256,640]{1,0:T(8,128)(2,1)}, bf16[256,640]{1,0:T(8,128)(2,1)}, f32[1,128]{1,0:T(1,128)}, f32[1,128]{1,0:T(1,128)}) custom-call(bf16[256,640]{1,0:T(8,128)(2,1)S(1)} %get-tuple-element.14.q, bf16[256,640]{1,0:T(8,128)(2,1)S(1)} %get-tuple-element.15.k, bf16[256,640]{1,0:T(8,128)(2,1)S(1)} %get-tuple-element.16.v, ...), custom_call_target="tpu_custom_call" | custom-call | tf_op jit(solution)/shard_map/pallas_call | solution.py:399

commit v5 on v4

--- a/solution.py
+++ b/solution.py
@@ -30,12 +30,12 @@
     "G0 F2 V0 B0",
     "C1 Q4 G1 B1",
     "F3 C2 G2 B2",
-    "F4 D0 D1 H0",
-    "C3 G3 B3 C4",
-    "G4 B4 A0 D2",
-    "H1 H2 H3 H4",
-    "E0 A1 D3 E1",
-    "W0 W1 A2 D4",
+    "F4 D0 C3 G3",
+    "B3 D1 C4 G4",
+    "B4 A0 D2 H0",
+    "H1 E0 A1 D3",
+    "H2 H3 E1 W0",
+    "W1 A2 D4 H4",
     "E2 W2 E3 W3",
     "E4 W4 A3",
 )
@@ -53,7 +53,7 @@
     oq_hbm, ok_hbm, ov_hbm, ogain_ref,
     raw_q, raw_k, qn, kn, vn, gn, rq, rg,
     q_hat, q_inv, k_hat, k_inv, prob, dprob, near_out, near_in,
-    stat_out, stat_in, cross_in, fin_own, dq_own, dk_sum, dv_sum, dq_out, dq_in, oq, ok, ov, acc,
+    stat_out, stat_in, cross_in, fin_own, fin_far, dq_own, dk_sum, dv_sum, dq_out, dq_in, oq, ok, ov, acc,
     sum_a, sum_b, sum_c,
     load_sem, store_sem, qs, qr, gs, gr, ss, sr, ns, nr, xs, xr, ds, dr, as_, ar,
 ):
@@ -134,7 +134,7 @@
     def send(h):
         if h == 0:
             pl.semaphore_wait(barrier, PEERS)
-        for i in (1, 0):
+        for i in (0, 1):
             g_copy(h, i).start()
             q_copy(h, i).start()
 
@@ -216,10 +216,13 @@
     def one_back(h, slot, query, grad, share, row_dot):
         w = prob[slot, h] * share
         ds_t = (w * (dprob[slot, h] - row_dot) * FACTOR).astype(jnp.bfloat16)
-        dv = mm(w.astype(jnp.bfloat16), grad, NN)
         dk = mm(ds_t, query, NN)
         dq = mm(ds_t, kn[h], TN)
-        return dq, dk, dv
+        return dq, dk
+
+    def value_back(h, slot, grad, share):
+        w = prob[slot, h] * share
+        return mm(w.astype(jnp.bfloat16), grad, NN)
 
     def norm_back(hat, inv, gain, grad):
         gg = grad * gain
@@ -236,27 +239,31 @@
         return pltpu.make_async_copy(src.at[h], dst.at[:, columns(h)], store_sem.at[slot, h])
 
     def near_back(h):
-        dq, dk, dv = one_back(h, 0, qn[h], gn[h], fin_own[h, 0:1], fin_own[h, 1:2])
+        share = fin_own[h, 0:1]
+        dq, dk = one_back(h, 0, qn[h], gn[h], share, fin_own[h, 1:2])
         dq_own[h] = dq
         dk_sum[h] = dk
-        dv_sum[h] = dv
+        dv_sum[h] = value_back(h, 0, gn[h], share)
         acc[0] += fold(dq * q_hat[h])
 
     def far_back(h):
-        gk, gv = dk_sum[h], dv_sum[h]
+        gk = dk_sum[h]
         x_copy(h).wait_recv()
         for i in (1, 0):
             share, row_dot = far_shares(h, i)
-            dq, dk, dv = one_back(h, i + 1, rq[i, h], rg[i, h], share, row_dot)
+            fin_far[h, i : i + 1] = share
+            dq, dk = one_back(h, i + 1, rq[i, h], rg[i, h], share, row_dot)
             dq_out[i, h] = dq.astype(jnp.bfloat16)
             acc[1] += fold(dq * rq[i, h].astype(jnp.float32))
-            gk, gv = gk + dk, gv + dv
+            gk = gk + dk
         dk_sum[h] = gk
-        dv_sum[h] = gv
         acc[2] += fold(gk * k_hat[h])
 
     def write_kv(h):
-        ov[h] = dv_sum[h].astype(jnp.bfloat16)
+        gv = dv_sum[h]
+        for i in range(BITS):
+            gv = gv + value_back(h, i + 1, rg[i, h], fin_far[h, i : i + 1])
+        ov[h] = gv.astype(jnp.bfloat16)
         store(ov, ov_hbm, 2, h).start()
         ok[h] = norm_back(k_hat[h], k_inv[h], gain_k, dk_sum[h])
         store(ok, ok_hbm, 1, h).start()
@@ -370,7 +377,7 @@
             vmem(*square), vmem(*square),
             vmem(HEADS, 4, ROWS), vmem(BITS, HEADS, 4, ROWS),
             vmem(HEADS, BITS, 2, ROWS), vmem(HEADS, BITS, 2, ROWS), vmem(HEADS, BITS, 2, ROWS),
-            vmem(HEADS, 2, ROWS),
+            vmem(HEADS, 2, ROWS), vmem(HEADS, BITS, ROWS),
             vmem(*tile), vmem(*tile), vmem(*tile), vmem(BITS, *tile, dtype=low), vmem(BITS, *tile, dtype=low),
             vmem(*tile, dtype=low), vmem(*tile, dtype=low), vmem(*tile, dtype=low),
             vmem(3, 8, HEAD_DIM),

time: 61.8 us -> 61.2 us (level)
  Pallas kernels: 60.3 us -> 59.4 us
    pallas_call x1, Pallas kernels: 59.3 us -> 58.5 us  [body(): pl.pallas_call(kernel, out_shape=(pltpu.VMEM((ROWS, HEADS * HEAD_DIM), lo...]
where the time goes in v5:
time: 61.2 us; the launch traced here: 60.7 us
  Pallas kernels  59.4 us (97%)
  between operations  1.29 us (2%)
    pallas_call x1, Pallas kernels, body(): pl.pallas_call(kernel, out_shape=(pltpu.VMEM((ROWS, HEADS * HEAD_DIM), lo...  58.5 us

profile of v5, /device:TPU:1, one launch (start us, length us, event | category | flops | bytes accessed | tf_op | source)
XLA Modules:
  0.0 60.7 jit_solution(4616322436374805799)
XLA Ops:
  1.3 58.5 %shard_map.119 = (bf16[256,640]{1,0:T(8,128)(2,1)S(1)}, bf16[256,640]{1,0:T(8,128)(2,1)S(1)}, bf16[256,640]{1,0:T(8,128)(2,1)S(1)}, f32[2,128]{1,0:T(2,128)S(1)}) custom-call(bf16[256,640]{1,0:T(8,128)(2,1)} %q_hbm.1, bf16[256,640]{1,0:T(8,128)(2,1)} %k_hbm.1, bf16[256,640]{1,0:T(8,128)(2,1)} %v_hbm.1, bf16[256,640]{1,0:T(8,128)(2,1)} %g_hbm.1, ...), custom_call_target="tpu_custom_call" | custom-call | flops 1258291200 | bytes 2293760 | tf_op jit(solution)/shard_map/pallas_call | solution.py:367
  59.7 1.0 %shard_map.120 = (bf16[256,640]{1,0:T(8,128)(2,1)}, bf16[256,640]{1,0:T(8,128)(2,1)}, bf16[256,640]{1,0:T(8,128)(2,1)}, f32[1,128]{1,0:T(1,128)}, f32[1,128]{1,0:T(1,128)}) custom-call(bf16[256,640]{1,0:T(8,128)(2,1)S(1)} %get-tuple-element.14.q, bf16[256,640]{1,0:T(8,128)(2,1)S(1)} %get-tuple-element.15.k, bf16[256,640]{1,0:T(8,128)(2,1)S(1)} %get-tuple-element.16.v, ...), custom_call_target="tpu_custom_call" | custom-call | tf_op jit(solution)/shard_map/pallas_call | solution.py:406

commit v6 on v5

--- a/solution.py
+++ b/solution.py
@@ -51,11 +51,11 @@
 def kernel(
     q_hbm, k_hbm, v_hbm, g_hbm, gain_q_ref, gain_k_ref, blocks_ref, count_ref,
     oq_hbm, ok_hbm, ov_hbm, ogain_ref,
-    raw_q, raw_k, qn, kn, vn, gn, rq, rg,
+    raw_q, raw_k, qg, kn, vn, rqg,
     q_hat, q_inv, k_hat, k_inv, prob, dprob, near_out, near_in,
     stat_out, stat_in, cross_in, fin_own, fin_far, dq_own, dk_sum, dv_sum, dq_out, dq_in, oq, ok, ov, acc,
     sum_a, sum_b, sum_c,
-    load_sem, store_sem, qs, qr, gs, gr, ss, sr, ns, nr, xs, xr, ds, dr, as_, ar,
+    load_sem, store_sem, qs, qr, ss, sr, ns, nr, xs, xr, ds, dr, as_, ar,
 ):
     place = lax.axis_index("ctx")
     column = lax.axis_index("head")
@@ -78,8 +78,13 @@
             src.at[:, h * HEAD_DIM : (h + 1) * HEAD_DIM], dst.at[h], load_sem.at[slot, h]
         )
 
+    def load_g(h):
+        return pltpu.make_async_copy(
+            g_hbm.at[:, h * HEAD_DIM : (h + 1) * HEAD_DIM], qg.at[h, 1], load_sem.at[0, h]
+        )
+
     for h in range(HEADS):
-        load(g_hbm, gn, 0, h).start()
+        load_g(h).start()
         load(q_hbm, raw_q, 1, h).start()
 
     def remote(src, dst, send, recv, peer):
@@ -89,10 +94,7 @@
         )
 
     def q_copy(h, i):
-        return remote(qn.at[h], rq.at[i, h], qs.at[i, h], qr.at[i, h], {"ctx": partners[i]})
-
-    def g_copy(h, i):
-        return remote(gn.at[h], rg.at[i, h], gs.at[i, h], gr.at[i, h], {"ctx": partners[i]})
+        return remote(qg.at[h], rqg.at[i, h], qs.at[i, h], qr.at[i, h], {"ctx": partners[i]})
 
     def s_copy(h, i):
         return remote(stat_out.at[h, i], stat_in.at[h, i], ss.at[i, h], sr.at[i, h], {"ctx": partners[i]})
@@ -124,18 +126,20 @@
         x_hat = x * inverse
         hat[h] = x_hat
         inv[h] = jnp.broadcast_to(inverse, x.shape)
-        normed[h] = (x_hat * gain).astype(jnp.bfloat16)
+        if normed is qg:
+            normed[h, 0] = (x_hat * gain).astype(jnp.bfloat16)
+        else:
+            normed[h] = (x_hat * gain).astype(jnp.bfloat16)
 
     def norm_query(h):
         load(q_hbm, raw_q, 1, h).wait()
-        load(g_hbm, gn, 0, h).wait()
-        norm(raw_q, gain_q, q_hat, q_inv, qn, h)
+        load_g(h).wait()
+        norm(raw_q, gain_q, q_hat, q_inv, qg, h)
 
     def send(h):
         if h == 0:
             pl.semaphore_wait(barrier, PEERS)
         for i in (0, 1):
-            g_copy(h, i).start()
             q_copy(h, i).start()
 
     def load_kv(h):
@@ -163,9 +167,8 @@
 
     def far_forward(h):
         for i in (0, 1):
-            g_copy(h, i).wait_recv()
             q_copy(h, i).wait_recv()
-            log, dot = forward(h, i + 1, rq[i, h], rg[i, h])
+            log, dot = forward(h, i + 1, rqg[i, h, 0], rqg[i, h, 1])
             stat_out[h, i, 0:1] = jnp.where(off[i] > 0.5, FLOOR_LOG, log)
             stat_out[h, i, 1:2] = dot
             if i == 1:
@@ -173,7 +176,7 @@
             s_copy(h, i).start()
 
     def near_forward(h):
-        log, dot = forward(h, 0, qn[h], gn[h])
+        log, dot = forward(h, 0, qg[h, 0], qg[h, 1])
         near_out[h, 0:1] = log
         near_out[h, 1:2] = dot
         for i in range(BITS):
@@ -240,10 +243,10 @@
 
     def near_back(h):
         share = fin_own[h, 0:1]
-        dq, dk = one_back(h, 0, qn[h], gn[h], share, fin_own[h, 1:2])
+        dq, dk = one_back(h, 0, qg[h, 0], qg[h, 1], share, fin_own[h, 1:2])
         dq_own[h] = dq
         dk_sum[h] = dk
-        dv_sum[h] = value_back(h, 0, gn[h], share)
+        dv_sum[h] = value_back(h, 0, qg[h, 1], share)
         acc[0] += fold(dq * q_hat[h])
 
     def far_back(h):
@@ -252,9 +255,9 @@
         for i in (1, 0):
             share, row_dot = far_shares(h, i)
             fin_far[h, i : i + 1] = share
-            dq, dk = one_back(h, i + 1, rq[i, h], rg[i, h], share, row_dot)
+            dq, dk = one_back(h, i + 1, rqg[i, h, 0], rqg[i, h, 1], share, row_dot)
             dq_out[i, h] = dq.astype(jnp.bfloat16)
-            acc[1] += fold(dq * rq[i, h].astype(jnp.float32))
+            acc[1] += fold(dq * rqg[i, h, 0].astype(jnp.float32))
             gk = gk + dk
         dk_sum[h] = gk
         acc[2] += fold(gk * k_hat[h])
@@ -262,7 +265,7 @@
     def write_kv(h):
         gv = dv_sum[h]
         for i in range(BITS):
-            gv = gv + value_back(h, i + 1, rg[i, h], fin_far[h, i : i + 1])
+            gv = gv + value_back(h, i + 1, rqg[i, h, 1], fin_far[h, i : i + 1])
         ov[h] = gv.astype(jnp.bfloat16)
         store(ov, ov_hbm, 2, h).start()
         ok[h] = norm_back(k_hat[h], k_inv[h], gain_k, dk_sum[h])
@@ -321,7 +324,7 @@
 
     def wait_sent(h):
         for i in range(BITS):
-            for copy in (q_copy, g_copy, s_copy, d_copy):
+            for copy in (q_copy, s_copy, d_copy):
                 copy(h, i).wait_send()
         x_copy(h).wait_send()
         if h == 0:
@@ -371,8 +374,8 @@
         out_specs=(any_space, any_space, any_space, in_vmem),
         scratch_shapes=[
             vmem(*tile, dtype=low), vmem(*tile, dtype=low),
-            vmem(*tile, dtype=low), vmem(*tile, dtype=low), vmem(*tile, dtype=low), vmem(*tile, dtype=low),
-            vmem(BITS, *tile, dtype=low), vmem(BITS, *tile, dtype=low),
+            vmem(HEADS, 2, ROWS, HEAD_DIM, dtype=low), vmem(*tile, dtype=low), vmem(*tile, dtype=low),
+            vmem(BITS, HEADS, 2, ROWS, HEAD_DIM, dtype=low),
             vmem(*tile), vmem(*tile), vmem(*tile), vmem(*tile),
             vmem(*square), vmem(*square),
             vmem(HEADS, 4, ROWS), vmem(BITS, HEADS, 4, ROWS),
@@ -383,7 +386,7 @@
             vmem(3, 8, HEAD_DIM),
             vmem(HEAD_DEVS, 2, HEAD_DIM), vmem(Y_DEVS, 2, HEAD_DIM), vmem(Z_DEVS, 2, HEAD_DIM),
             pltpu.SemaphoreType.DMA((4, HEADS)), pltpu.SemaphoreType.DMA((3, HEADS)),
-            pair, pair, pair, pair, pair, pair,
+            pair, pair, pair, pair,
             pltpu.SemaphoreType.DMA((BITS,)), pltpu.SemaphoreType.DMA((BITS,)),
             pltpu.SemaphoreType.DMA((HEADS,)), pltpu.SemaphoreType.DMA((HEADS,)), pair, pair,
             pltpu.SemaphoreType.DMA((PEERS,)), pltpu.SemaphoreType.DMA((PEERS,)),

time: 61.2 us -> 61 us (level)
  no operation moved by 1% of the time
where the time goes in v6:
time: 61 us; the launch traced here: 60.6 us
  Pallas kernels  59.3 us (97%)
  between operations  1.29 us (2%)
    pallas_call x1, Pallas kernels, body(): pl.pallas_call(kernel, out_shape=(pltpu.VMEM((ROWS, HEADS * HEAD_DIM), lo...  58.3 us

profile of v6, /device:TPU:1, one launch (start us, length us, event | category | flops | bytes accessed | tf_op | source)
XLA Modules:
  0.0 60.6 jit_solution(11018071843047684662)
XLA Ops:
  1.3 58.3 %shard_map.119 = (bf16[256,640]{1,0:T(8,128)(2,1)S(1)}, bf16[256,640]{1,0:T(8,128)(2,1)S(1)}, bf16[256,640]{1,0:T(8,128)(2,1)S(1)}, f32[2,128]{1,0:T(2,128)S(1)}) custom-call(bf16[256,640]{1,0:T(8,128)(2,1)} %q_hbm.1, bf16[256,640]{1,0:T(8,128)(2,1)} %k_hbm.1, bf16[256,640]{1,0:T(8,128)(2,1)} %v_hbm.1, bf16[256,640]{1,0:T(8,128)(2,1)} %g_hbm.1, ...), custom_call_target="tpu_custom_call" | custom-call | flops 1258291200 | bytes 2293760 | tf_op jit(solution)/shard_map/pallas_call | solution.py:370
  59.6 1.0 %shard_map.120 = (bf16[256,640]{1,0:T(8,128)(2,1)}, bf16[256,640]{1,0:T(8,128)(2,1)}, bf16[256,640]{1,0:T(8,128)(2,1)}, f32[1,128]{1,0:T(1,128)}, f32[1,128]{1,0:T(1,128)}) custom-call(bf16[256,640]{1,0:T(8,128)(2,1)S(1)} %get-tuple-element.14.q, bf16[256,640]{1,0:T(8,128)(2,1)S(1)} %get-tuple-element.15.k, bf16[256,640]{1,0:T(8,128)(2,1)S(1)} %get-tuple-element.16.v, ...), custom_call_target="tpu_custom_call" | custom-call | tf_op jit(solution)/shard_map/pallas_call | solution.py:409

commit v7 on v5

--- a/solution.py
+++ b/solution.py
@@ -127,15 +127,20 @@
         normed[h] = (x_hat * gain).astype(jnp.bfloat16)
 
     def norm_query(h):
+        if h == 0:
+            load(g_hbm, gn, 0, h).wait()
+            pl.semaphore_wait(barrier, PEERS)
+            for i in (0, 1):
+                g_copy(h, i).start()
         load(q_hbm, raw_q, 1, h).wait()
-        load(g_hbm, gn, 0, h).wait()
+        if h > 0:
+            load(g_hbm, gn, 0, h).wait()
         norm(raw_q, gain_q, q_hat, q_inv, qn, h)
 
     def send(h):
-        if h == 0:
-            pl.semaphore_wait(barrier, PEERS)
         for i in (0, 1):
-            g_copy(h, i).start()
+            if h > 0:
+                g_copy(h, i).start()
             q_copy(h, i).start()
 
     def load_kv(h):

time: 61.2 us -> 61.1 us (level)
  no operation moved by 1% of the time
where the time goes in v7:
time: 61.1 us; the launch traced here: 60.7 us
  Pallas kernels  59.4 us (97%)
  between operations  1.29 us (2%)
    pallas_call x1, Pallas kernels, body(): pl.pallas_call(kernel, out_shape=(pltpu.VMEM((ROWS, HEADS * HEAD_DIM), lo...  58.5 us

profile of v7, /device:TPU:1, one launch (start us, length us, event | category | flops | bytes accessed | tf_op | source)
XLA Modules:
  0.0 60.7 jit_solution(485279147812801786)
XLA Ops:
  1.3 58.5 %shard_map.119 = (bf16[256,640]{1,0:T(8,128)(2,1)S(1)}, bf16[256,640]{1,0:T(8,128)(2,1)S(1)}, bf16[256,640]{1,0:T(8,128)(2,1)S(1)}, f32[2,128]{1,0:T(2,128)S(1)}) custom-call(bf16[256,640]{1,0:T(8,128)(2,1)} %q_hbm.1, bf16[256,640]{1,0:T(8,128)(2,1)} %k_hbm.1, bf16[256,640]{1,0:T(8,128)(2,1)} %v_hbm.1, bf16[256,640]{1,0:T(8,128)(2,1)} %g_hbm.1, ...), custom_call_target="tpu_custom_call" | custom-call | flops 1258291200 | bytes 2293760 | tf_op jit(solution)/shard_map/pallas_call | solution.py:372
  59.7 1.0 %shard_map.120 = (bf16[256,640]{1,0:T(8,128)(2,1)}, bf16[256,640]{1,0:T(8,128)(2,1)}, bf16[256,640]{1,0:T(8,128)(2,1)}, f32[1,128]{1,0:T(1,128)}, f32[1,128]{1,0:T(1,128)}) custom-call(bf16[256,640]{1,0:T(8,128)(2,1)S(1)} %get-tuple-element.14.q, bf16[256,640]{1,0:T(8,128)(2,1)S(1)} %get-tuple-element.15.k, bf16[256,640]{1,0:T(8,128)(2,1)S(1)} %get-tuple-element.16.v, ...), custom_call_target="tpu_custom_call" | custom-call | tf_op jit(solution)/shard_map/pallas_call | solution.py:411
